TPU v7x, 32 devices: a whole 2x2x4 slice. The times are simulated.
32 devices in a mesh: rep: 4 (over z), shard: 8 (over y, x, core).
Axes of the slice: x: 2, y: 2, z: 4, core: 2. Of those that a mesh axis runs over, the one named last changes fastest.
Arguments:
- tokens: bfloat16 [32, 256, 2048], P(('rep', 'shard')), may hold values from -6 to 6
- lengths: int32 [32], replicated, may hold values from 1 to 256, 6144 in all
- order: int32 [32], replicated, may hold values from 0 to 31, as said below
- norm_gain: bfloat16 [2, 2048], P(None, 'shard'), may hold values from 0.099609375 to 1.8984375
- in_proj: bfloat16 [2, 2048, 8512], P(None, 'shard'), may hold values from -0.125 to 0.125
- conv_weight: bfloat16 [2, 4, 4352], P(None, None, 'shard'), may hold values from -3 to 3
- conv_bias: bfloat16 [2, 4352], P(None, 'shard'), may hold values from -0.5 to 0.5
- dt_bias: bfloat16 [2, 64], P(None, 'shard'), may hold values from -6 to -2
- a_log: bfloat16 [2, 64], P(None, 'shard'), may hold values from 0 to 2.765625
- skip: bfloat16 [2, 64], P(None, 'shard'), may hold values from 0.5 to 1.5
- gate_norm: bfloat16 [2, 4096], P(None, 'shard'), may hold values from 0.099609375 to 1.8984375
- out_proj: bfloat16 [2, 4096, 2048], P(None, 'shard'), may hold values from -0.09375 to 0.09375
- cotangent: bfloat16 [32, 256, 2048], P(('rep', 'shard')), may hold values from -6 to 6
Outputs:
- output: bfloat16 [32, 256, 2048], P(('rep', 'shard'))
- grad_tokens: bfloat16 [32, 256, 2048], P(('rep', 'shard'))
- grad_norm_gain: float32 [2, 2048], P(None, 'shard')
- grad_in_proj: float32 [2, 2048, 8512], P(None, 'shard')
- grad_conv_weight: float32 [2, 4, 4352], P(None, None, 'shard')
- grad_conv_bias: float32 [2, 4352], P(None, 'shard')
- grad_dt_bias: float32 [2, 64], P(None, 'shard')
- grad_a_log: float32 [2, 64], P(None, 'shard')
- grad_skip: float32 [2, 64], P(None, 'shard')
- grad_gate_norm: float32 [2, 4096], P(None, 'shard')
- grad_out_proj: float32 [2, 4096, 2048], P(None, 'shard')
Inputs may be any that keep to these rules, and one draw needn't show every extreme that they name: `lengths`: each length counts the valid leading positions of its sequence; one sequence fills all 256 positions in every draw. order is a permutation of the 32 sequences that maps each aligned block of 8 slots starting at a multiple of 8 onto the sequences with the same indices as a set.
All inputs are finite; a program needn't handle non-finite values.
Results may differ from a plain program's by a relative error of at most 0.02.
Values may be sent and summed in bfloat16 or wider, within the bound.
A program may use at most 768 MiB of HBM per device.

v0:
```python
import jax
import jax.numpy as jnp
from jax import lax
from jax.sharding import PartitionSpec as P

SPAN = 256
LAYERS = 2


EPS = 1e-05
HIGH = lax.Precision.HIGHEST


def rms_scale(stream, gain):
    return stream * lax.rsqrt(jnp.mean(stream * stream, axis=-1, keepdims=True) + EPS) * gain


def block_step(state_in, block):
    inputs_b, keys_b, queries_b, delta_b, logdec_b = block
    cumul = jnp.cumsum(logdec_b, axis=0)
    count = cumul.shape[0]
    causal = (jnp.arange(count)[:, None] >= jnp.arange(count)[None, :])[:, :, None]
    spread = cumul[:, None, :] - cumul[None, :, :]
    decay = jnp.where(causal, jnp.exp(jnp.where(causal, spread, 0.0)), 0.0)
    scores = jnp.dot(queries_b, keys_b.T, precision=HIGH)
    weights = scores[:, :, None] * decay * delta_b[None, :, :]
    intra = jnp.einsum("tsh,shp->thp", weights, inputs_b, precision=HIGH)
    inter = (
        jnp.einsum("tn,hpn->thp", queries_b, state_in, precision=HIGH) * jnp.exp(cumul)[:, :, None]
    )
    tail = jnp.exp(cumul[-1][None, :] - cumul) * delta_b
    carried = jnp.exp(cumul[-1])[:, None, None] * state_in + jnp.einsum(
        "sh,sn,shp->hpn", tail, keys_b, inputs_b, precision=HIGH
    )
    return (carried, intra + inter)


def scan_blocks(inputs, keys, queries, delta, logdec):
    rows, heads, headdim = inputs.shape
    state = keys.shape[1]
    blocks = rows // SPAN
    packed = (
        inputs.reshape(blocks, SPAN, heads, headdim),
        keys.reshape(blocks, SPAN, state),
        queries.reshape(blocks, SPAN, state),
        delta.reshape(blocks, SPAN, heads),
        logdec.reshape(blocks, SPAN, heads),
    )
    start = jnp.zeros((heads, headdim, state), jnp.float32)
    final, outputs = lax.scan(jax.checkpoint(block_step), start, packed)
    return outputs.reshape(rows, heads, headdim)


def mixer(projected, conv_weight, conv_bias, dt_bias, a_log, skip, gate_norm):
    inner = gate_norm.shape[0]
    heads = dt_bias.shape[0]
    headdim = inner // heads
    channels = conv_bias.shape[0]
    state = (channels - inner) // 2
    taps = conv_weight.shape[0]
    rows = projected.shape[0]
    gate_part = projected[:, :inner]
    conv_in = projected[:, inner : inner + channels]
    step_raw = projected[:, inner + channels :]
    padded = jnp.pad(conv_in, ((taps - 1, 0), (0, 0)))
    convolved = conv_bias + padded[0:rows] * conv_weight[0]
    for offset in range(1, taps):
        convolved = convolved + padded[offset : offset + rows] * conv_weight[offset]
    active = jax.nn.silu(convolved)
    inputs = active[:, :inner].reshape(rows, heads, headdim)
    keys = active[:, inner : inner + state]
    queries = active[:, inner + state :]
    delta = jax.nn.softplus(step_raw + dt_bias)
    logdec = -jnp.exp(a_log) * delta
    mixed = scan_blocks(inputs, keys, queries, delta, logdec) + skip[None, :, None] * inputs
    gated = mixed.reshape(rows, inner) * jax.nn.silu(gate_part)
    return rms_scale(gated, gate_norm)


def pick_one(wanted, carry, piece, start):
    count = piece.shape[0]
    local = jnp.clip(wanted, 0, count - 1)
    found = (wanted >= start) & (wanted < start + count)
    return jnp.where(found, lax.dynamic_slice_in_dim(piece, local, 1, 0), carry)


def pick_pair(wanted, carry, pieces, start):
    count = pieces[0].shape[0]
    local = jnp.clip(wanted, 0, count - 1)
    found = (wanted >= start) & (wanted < start + count)
    first = jnp.where(found, lax.dynamic_slice_in_dim(pieces[0], local, 1, 0), carry[0])
    second = jnp.where(found, lax.dynamic_slice_in_dim(pieces[1], local, 1, 0), carry[1])
    return (first, second)


def fetch_forward(pieces):
    return (
        lax.all_gather(pieces[0], "shard", axis=0, tiled=True),
        lax.all_gather(pieces[1], "shard", axis=0, tiled=True),
        lax.all_gather(pieces[2], "shard", axis=1, tiled=True),
        lax.all_gather(pieces[3], "shard", axis=0, tiled=True),
        lax.all_gather(pieces[4], "shard", axis=0, tiled=True),
        lax.all_gather(pieces[5], "shard", axis=0, tiled=True),
        lax.all_gather(pieces[6], "shard", axis=0, tiled=True),
        lax.all_gather(pieces[7], "shard", axis=0, tiled=True),
        lax.all_gather(pieces[8], "shard", axis=0, tiled=True),
    )


def reduce_grads(small, normed, grad_proj, gnorm, gbranch):
    owners = lax.axis_size("shard")
    owner = lax.axis_index("shard")
    width_part = normed.shape[1] // owners
    inner_part = gnorm.shape[1] // owners
    normed_piece = lax.all_gather(normed, "shard", axis=0, tiled=True)
    proj_piece = lax.all_gather(grad_proj, "shard", axis=0, tiled=True)
    gnorm_piece = lax.all_gather(gnorm, "shard", axis=0, tiled=True)
    branch_piece = lax.all_gather(gbranch, "shard", axis=0, tiled=True)
    rows_in = lax.dynamic_slice_in_dim(normed_piece, owner * width_part, width_part, 1)
    rows_out = lax.dynamic_slice_in_dim(gnorm_piece, owner * inner_part, inner_part, 1)
    grad_in_part = jnp.einsum("ta,tp->ap", rows_in, proj_piece, preferred_element_type=jnp.float32)
    grad_out_part = jnp.einsum(
        "ti,td->id", rows_out, branch_piece, preferred_element_type=jnp.float32
    )
    parted_small = (
        lax.psum_scatter(
            small[0].astype(jnp.bfloat16), "shard", scatter_dimension=0, tiled=True
        ).astype(jnp.float32),
        lax.psum_scatter(
            small[1].astype(jnp.bfloat16), "shard", scatter_dimension=1, tiled=True
        ).astype(jnp.float32),
        lax.psum_scatter(
            small[2].astype(jnp.bfloat16), "shard", scatter_dimension=0, tiled=True
        ).astype(jnp.float32),
        lax.psum_scatter(
            small[3].astype(jnp.bfloat16), "shard", scatter_dimension=0, tiled=True
        ).astype(jnp.float32),
        lax.psum_scatter(
            small[4].astype(jnp.bfloat16), "shard", scatter_dimension=0, tiled=True
        ).astype(jnp.float32),
        lax.psum_scatter(
            small[5].astype(jnp.bfloat16), "shard", scatter_dimension=0, tiled=True
        ).astype(jnp.float32),
        lax.psum_scatter(
            small[6].astype(jnp.bfloat16), "shard", scatter_dimension=0, tiled=True
        ).astype(jnp.float32),
    )
    parted = (
        parted_small[0],
        grad_in_part,
        parted_small[1],
        parted_small[2],
        parted_small[3],
        parted_small[4],
        parted_small[5],
        parted_small[6],
        grad_out_part,
    )
    return (
        lax.psum(parted[0].astype(jnp.bfloat16), "rep").astype(jnp.float32),
        lax.psum(parted[1].astype(jnp.bfloat16), "rep").astype(jnp.float32),
        lax.psum(parted[2].astype(jnp.bfloat16), "rep").astype(jnp.float32),
        lax.psum(parted[3].astype(jnp.bfloat16), "rep").astype(jnp.float32),
        lax.psum(parted[4].astype(jnp.bfloat16), "rep").astype(jnp.float32),
        lax.psum(parted[5].astype(jnp.bfloat16), "rep").astype(jnp.float32),
        lax.psum(parted[6].astype(jnp.bfloat16), "rep").astype(jnp.float32),
        lax.psum(parted[7].astype(jnp.bfloat16), "rep").astype(jnp.float32),
        lax.psum(parted[8].astype(jnp.bfloat16), "rep").astype(jnp.float32),
    )


def body(
    tokens,
    lengths,
    order,
    norm_gain,
    in_proj,
    conv_weight,
    conv_bias,
    dt_bias,
    a_log,
    skip,
    gate_norm,
    out_proj,
    cotangent,
):
    group = lax.axis_size("shard")
    base = lax.axis_index("rep") * group
    slot = base + lax.axis_index("shard")
    held = order[slot]
    listing = jnp.arange(order.shape[0])
    source = jnp.sum(jnp.where(order == slot, listing, 0))
    stream = tokens[0].astype(jnp.float32)
    rows = stream.shape[0]
    mask = (jnp.arange(rows) < lengths[held]).astype(jnp.float32)[:, None]
    shards = (norm_gain, in_proj, conv_weight, conv_bias, dt_bias, a_log, skip, gate_norm, out_proj)

    def layer_shards(layer):
        return tuple((entry[layer] for entry in shards))

    saved = []
    kept = []
    for layer in range(LAYERS):
        gathered = fetch_forward(layer_shards(layer))
        normed = rms_scale(stream, gathered[0].astype(jnp.float32)).astype(jnp.bfloat16)
        projected = jnp.dot(normed, gathered[1], preferred_element_type=jnp.float32)
        small = tuple((entry.astype(jnp.float32) for entry in gathered[2:8]))
        gnorm = mixer(projected, *small).astype(jnp.bfloat16)
        branch = jnp.dot(gnorm, gathered[8], preferred_element_type=jnp.float32)
        saved.append((stream, normed, projected))
        kept.append(gathered)
        stream = stream + mask * branch
    output_slot = stream.astype(jnp.bfloat16)[None]
    placed = pick_one(
        held - base,
        jnp.zeros_like(cotangent),
        lax.all_gather(cotangent, "shard", axis=0, tiled=True),
        jnp.int32(0),
    )
    flow = placed[0].astype(jnp.float32)
    owned = [None] * LAYERS
    for layer in reversed(range(LAYERS)):
        gathered = kept[layer]
        layer_in, normed, projected = saved[layer]
        gain_value = gathered[0].astype(jnp.float32)
        small = tuple((entry.astype(jnp.float32) for entry in gathered[2:8]))
        gnorm_full, pull_mixer = jax.vjp(mixer, projected, *small)
        gnorm = gnorm_full.astype(jnp.bfloat16)
        gbranch = (mask * flow).astype(jnp.bfloat16)
        grad_gnorm = jnp.einsum(
            "td,id->ti", gbranch, gathered[8], preferred_element_type=jnp.float32
        )
        mixer_grads = pull_mixer(grad_gnorm)
        grad_proj = mixer_grads[0].astype(jnp.bfloat16)
        grad_normed = jnp.einsum(
            "tp,ap->ta", grad_proj, gathered[1], preferred_element_type=jnp.float32
        )
        normed_again, pull_norm = jax.vjp(rms_scale, layer_in, gain_value)
        grad_stream, grad_gain = pull_norm(grad_normed)
        flow = flow + grad_stream
        small_grads = (
            grad_gain,
            mixer_grads[1],
            mixer_grads[2],
            mixer_grads[3],
            mixer_grads[4],
            mixer_grads[5],
            mixer_grads[6],
        )
        owned[layer] = reduce_grads(small_grads, normed, grad_proj, gnorm, gbranch)
    grad_slot = flow.astype(jnp.bfloat16)[None]
    output, grad_tokens = pick_pair(
        source - base,
        (jnp.zeros_like(output_slot), jnp.zeros_like(grad_slot)),
        (
            lax.all_gather(output_slot, "shard", axis=0, tiled=True),
            lax.all_gather(grad_slot, "shard", axis=0, tiled=True),
        ),
        jnp.int32(0),
    )
    stacked = tuple(
        (jnp.stack([owned[layer][index] for layer in range(LAYERS)]) for index in range(9))
    )
    return (output, grad_tokens) + stacked


def solution(mesh):
    in_specs = (
        P(("rep", "shard"), None, None),
        P(),
        P(),
        P(None, "shard"),
        P(None, "shard", None),
        P(None, None, "shard"),
        P(None, "shard"),
        P(None, "shard"),
        P(None, "shard"),
        P(None, "shard"),
        P(None, "shard"),
        P(None, "shard", None),
        P(("rep", "shard"), None, None),
    )
    out_specs = (
        P(("rep", "shard"), None, None),
        P(("rep", "shard"), None, None),
        P(None, "shard"),
        P(None, "shard", None),
        P(None, None, "shard"),
        P(None, "shard"),
        P(None, "shard"),
        P(None, "shard"),
        P(None, "shard"),
        P(None, "shard"),
        P(None, "shard", None),
    )
    return jax.shard_map(body, mesh=mesh, in_specs=in_specs, out_specs=out_specs, check_vma=False)
```

profile of v0, /device:TPU:0, one launch (start us, length us, event | category | flops | bytes accessed | tf_op | source)
XLA Modules:
  0.0 2237.7 jit_solution(903253985773716459)
XLA Ops:
  26.7 26.6 %all-reduce.55 = (bf16[4352]{0:T(1024)(128)(2,1)S(1)}, bf16[64]{0:T(256)(128)(2,1)S(1)}, bf16[64]{0:T(256)(128)(2,1)}, bf16[64]{0:T(256)(128)(2,1)S(1)}, bf16[43...) all-reduce(bf16[4352]{0:T(1024)(128)(2,1)S(1)} %dynamic-update-slic, ...), channel_id=2, replica_groups=mesh['rep'=4,'shard'=8] {'shard'}, use_global_device_ids=true, to_apply=%add.34 | all-reduce | flops 9088 | bytes 36352
  103.6 25.3 %all-gather.12 = bf16[1,4,4352]{1,0,2:T(2,128)(2,1)S(1)} all-gather(bf16[1,4,544]{1,0,2:T(2,128)(2,1)S(1)} %copy.395), channel_id=14, replica_groups=mesh['rep'=4,'shard'=8] {'shard'}, dimensions={2}, use_global_device_ids=true | all-gather | bytes 39168 | tf_op jit(solution)/shard_map/all_gather | solution.py:100
  147.0 90.0 %slice_reduce_fusion.7 = (f32[4352]{0:T(1024)S(1)}, f32[4352]{0:T(1024)S(1)}, f32[4352]{0:T(1024)S(1)}, f32[4352]{0:T(1024)S(1)}) fusion(f32[1,4,4352]{1,0,2:T(1,128)S(1)} %convert_element_type.270), kind=kLoop, calls=%fused_computation.202 | loop fusion | bytes 139264 | tf_op jit(solution)/shard_map/slice | solution.py:66
  237.1 90.2 %slice_reduce_fusion.3 = (f32[4352]{0:T(1024)S(1)}, f32[4352]{0:T(1024)S(1)}, f32[4352]{0:T(1024)S(1)}, f32[4352]{0:T(1024)S(1)}) fusion(f32[1,4,4352]{1,0,2:T(1,128)S(1)} %copy-done.2), kind=kLoop, calls=%fused_computation.198 | loop fusion | bytes 139264 | tf_op jit(solution)/shard_map/slice | solution.py:66
  383.2 21.2 bitcast_add_fusion.5
  410.2 23.5 %bitcast_add_fusion.1 = f32[256,64,64]{0,2,1:T(8,128)} fusion(f32[256,64,64]{0,2,1:T(8,128)} %copy-done.14, f32[256,64,64]{0,2,1:T(8,128)} %bitcast.351, f32[256,64]{0,1:T(8,128)S(1)} %copy.328, f32[256,64]{0,1:T(8,128)S(1)} %bitcast_bitcast_fusion.1, f32[256,256]{1,0:T(8,128)S(1)} %fusion.208, pred[256,256]{1,0:T(8,128)(4,1)S(1)} %iota_compare_fusion, ...), kind=kOutput, calls=%fused_computation.128 | convolution fusion | flops 3244294144 | bytes 13107200 | tf_op jit(solution)/shard_map/jvp()/while/body/eval_jaxpr/tsh,shp->thp/dot_general | solution.py:27
  461.0 60.3 %all-gather.58.cloned.1.call-done = bf16[1,2048,8512]{1,2,0:T(8,128)(2,1)} async-done(((bf16[1,256,8512]{1,2,0:T(8,128)(2,1)}), bf16[1,2048,8512]{1,2,0:T(8,128)(2,1)}) %all-gather.58.cloned.1.call-update) | async-done | bytes 34865168 | tf_op jit(solution)/shard_map/all_gather | solution.py:99
  574.1 21.0 bitcast_add_fusion.4
  600.8 23.5 %bitcast_add_fusion.3 = f32[256,64,64]{0,2,1:T(8,128)} fusion(f32[256,64,64]{0,2,1:T(8,128)} %copy-done.15, f32[256,64,64]{0,2,1:T(8,128)} %bitcast.356, f32[256,64]{0,1:T(8,128)S(1)} %copy.337, f32[256,64]{0,1:T(8,128)S(1)} %bitcast_bitcast_fusion, f32[256,256]{1,0:T(8,128)S(1)} %fusion.206, pred[256,256]{1,0:T(8,128)(4,1)S(1)} %iota_compare_fusion, ...), kind=kOutput, calls=%fused_computation.133 | convolution fusion | flops 3244294144 | bytes 13107200 | tf_op jit(solution)/shard_map/jvp()/while/body/eval_jaxpr/tsh,shp->thp/dot_general | solution.py:27
  638.0 20.6 multiply_reduce_fusion.12
  694.8 27.4 %fusion.35 = (f32[256,64]{0,1:T(8,128)S(1)}, f32[256,64]{0,1:T(8,128)S(1)}, f32[256,64]{0,1:T(8,128)}, f32[256,256]{1,0:T(8,128)S(1)}) fusion(f32[256,64]{0,1:T(8,128)S(1)} %copy.351, f32[256,64]{0,1:T(8,128)S(1)} %copy.347, f32[256,256]{1,0:T(8,128)S(1)} %copy-done.30, pred[256,256]{1,0:T(8,128)(4,1)S(1)} %copy-done.74, f32[256,64,64]{0,2,1:T(8,128)S(1)} %bitcast.360, ...), kind=kOutput, calls=%fused_computation.47 | convolution fusion | flops 3284025344 | bytes 9306112 | tf_op jit(solution)/shard_map/transpose(jvp())/while/body/eval_jaxpr/checkpoint/tsh,shp->thp/dot_general | solution.py:27
  878.9 28.7 %fusion.37 = (f32[256,64]{0,1:T(8,128)}, f32[256,64]{0,1:T(8,128)}, f32[256,64]{0,1:T(8,128)}, f32[256,256]{1,0:T(8,128)S(1)}) fusion(f32[256,64]{0,1:T(8,128)S(1)} %copy.370, f32[256,64]{0,1:T(8,128)S(1)} %copy.366, f32[256,256]{1,0:T(8,128)S(1)} %fusion.235, pred[256,256]{1,0:T(8,128)(4,1)S(1)} %copy-done.75, f32[256,64,64]{0,2,1:T(8,128)} %bitcast.352, ...), kind=kOutput, calls=%fused_computation.49 | convolution fusion | flops 3284025344 | bytes 9306112 | tf_op jit(solution)/shard_map/transpose(jvp())/while/body/eval_jaxpr/checkpoint/tsh,shp->thp/dot_general | solution.py:27
  1042.3 85.7 %all-gather.50.cloned.1.call-done = bf16[2048,4096]{1,0:T(8,128)(2,1)} async-done(((bf16[256,4096]{1,0:T(8,128)(2,1)}), bf16[2048,4096]{1,0:T(8,128)(2,1)}) %all-gather.50.cloned.1.call-update) | async-done | bytes 16777232 | tf_op jit(solution)/shard_map/all_gather | solution.py:117
  1138.0 46.2 %all-gather.42.cloned.1.call-done = bf16[2048,2048]{1,0:T(8,128)(2,1)} async-done(((bf16[256,2048]{1,0:T(8,128)(2,1)}), bf16[2048,2048]{1,0:T(8,128)(2,1)}) %all-gather.42.cloned.1.call-update) | async-done | bytes 8388624 | tf_op jit(solution)/shard_map/all_gather | solution.py:115
  1184.2 170.6 %all-gather.44.cloned.1.call-done = bf16[2048,8512]{1,0:T(8,128)(2,1)} async-done(((bf16[256,8512]{1,0:T(8,128)(2,1)}), bf16[2048,8512]{1,0:T(8,128)(2,1)}) %all-gather.44.cloned.1.call-update) | async-done | bytes 34865168 | tf_op jit(solution)/shard_map/all_gather | solution.py:116
  1354.8 20.8 fusion.33
  1375.6 36.0 %all-gather.38.cloned.1.call-done = bf16[2048,2048]{1,0:T(8,128)(2,1)} async-done(((bf16[256,2048]{1,0:T(8,128)(2,1)}), bf16[2048,2048]{1,0:T(8,128)(2,1)}) %all-gather.38.cloned.1.call-update) | async-done | bytes 8388624 | tf_op jit(solution)/shard_map/all_gather | solution.py:115
  1411.5 171.1 %all-gather.40.cloned.1.call-done = bf16[2048,8512]{1,0:T(8,128)(2,1)} async-done(((bf16[256,8512]{1,0:T(8,128)(2,1)}), bf16[2048,8512]{1,0:T(8,128)(2,1)}) %all-gather.40.cloned.1.call-update) | async-done | bytes 34865168 | tf_op jit(solution)/shard_map/all_gather | solution.py:116
  1582.7 20.4 fusion.32
  1608.0 24.2 %all-reduce.54 = (bf16[2048]{0:T(1024)(128)(2,1)S(1)}, bf16[2048]{0:T(1024)(128)(2,1)S(1)}, bf16[4352]{0:T(1024)(128)(2,1)S(1)}, bf16[4352]{0:T(1024)(128)(2,1)S...) all-reduce(bf16[2048]{0:T(1024)(128)(2,1)S(1)} %copy-done.97, ...), channel_id=23, replica_groups=mesh['rep'=4,'shard'=8] {'shard'}, use_global_device_ids=true, to_apply=%region_45.47.clone | all-reduce | flops 21376 | bytes 85504
  1634.2 27.8 %reduce-scatter.9.cloned.1.call-done = bf16[544,4]{1,0:T(8,128)(2,1)} async-done(((bf16[4352,4]{1,0:T(8,128)(2,1)}), bf16[544,4]{1,0:T(8,128)(2,1)}) %reduce-scatter.9.cloned.1.call-update) | async-done | bytes 4368
  1686.2 32.0 %all-gather.64.cloned.1.call-done = bf16[2048,2048]{1,0:T(8,128)(2,1)} async-done(((bf16[256,2048]{1,0:T(8,128)(2,1)}), bf16[2048,2048]{1,0:T(8,128)(2,1)}) %all-gather.64.cloned.1.call-update) | async-done | bytes 8388624 | tf_op jit(solution)/shard_map/all_gather | solution.py:257
  1720.4 53.9 %all-gather.62.cloned.1.call-done = bf16[2048,2048]{1,0:T(8,128)(2,1)} async-done(((bf16[256,2048]{1,0:T(8,128)(2,1)}), bf16[2048,2048]{1,0:T(8,128)(2,1)}) %all-gather.62.cloned.1.call-update) | async-done | bytes 8388624 | tf_op jit(solution)/shard_map/all_gather | solution.py:256
  1776.6 440.4 %all-reduce.60.cloned.1.call-done = (bf16[1,256,8512]{1,2,0:T(8,128)(2,1)}, bf16[1,256,8512]{1,2,0:T(8,128)(2,1)}, bf16[1,512,2048]{2,1,0:T(8,128)(2,1)}, bf16[1,512,2048]{2,1,0:T(8,128)(2,1)}) async-done(((bf16[1,256,8512]{1,2,0:T(8,128)(2,1)}, bf16[1,256,8512]{1,2,0:T(8,128)(2,1)}, bf16[1,512,2048]{2,1,0:T(8,128)(2,1)}, bf16[1,512,2048]{2,1,0:T(8,128)(2,1)}), (bf16[1,256,8512]{1,2,0:T(8,128)(2,1)}, ...) | async-done | bytes 12910608 | tf_op jit(solution)/shard_map/psum | solution.py:161
  (557 shorter events, 626.3 us)
Async XLA Ops:
  7.2 320.2 %all-gather.36.cloned.1.call-start = ((), (), s32[]{:S(2)}) async-start(), calls=%async_computation.2 | async-start | bytes 9437184 | tf_op jit(solution)/shard_map/all_gather | solution.py:217
  7.9 321.9 %all-gather.54.cloned.1.call-start = ((), (), s32[]{:S(2)}) async-start(), calls=%async_computation.11 | async-start | bytes 39223296 | tf_op jit(solution)/shard_map/all_gather | solution.py:99
  14.0 435.6 %all-gather.56.cloned.1.call-start = ((), (), s32[]{:S(2)}) async-start(), calls=%async_computation.12 | async-start | bytes 18874368 | tf_op jit(solution)/shard_map/all_gather | solution.py:106
  18.9 502.3 %all-gather.58.cloned.1.call-start = ((), (), s32[]{:S(2)}) async-start(), calls=%async_computation.13 | async-start | bytes 39223296 | tf_op jit(solution)/shard_map/all_gather | solution.py:99
  19.5 618.4 %all-gather.60.cloned.1.call-start = ((), (), s32[]{:S(2)}) async-start(), calls=%async_computation.14 | async-start | bytes 18874368 | tf_op jit(solution)/shard_map/all_gather | solution.py:106
  20.1 1012.1 %all-gather.48.cloned.1.call-start = ((), (), s32[]{:S(2)}) async-start(), calls=%async_computation.8 | async-start | bytes 9437184 | tf_op jit(solution)/shard_map/all_gather | solution.py:118
  145.2 304.4 %copy-start.101 = (f32[256]{0:T(256)}, f32[256]{0:T(256)S(1)}, u32[]{:S(2)}) copy-start(f32[256]{0:T(256)S(1)} %compare_convert_fusion) | copy-start | bytes 3076
  145.3 455.5 %copy-start.73 = (pred[256,256]{1,0:T(8,128)(4,1)}, pred[256,256]{1,0:T(8,128)(4,1)S(1)}, u32[]{:S(2)}) copy-start(pred[256,256]{1,0:T(8,128)(4,1)S(1)} %iota_compare_fusion) | copy-start | bytes 196612
  145.6 400.5 %copy-start.109 = (f32[64]{0:T(128)}, f32[64]{0:T(128)S(1)}, u32[]{:S(2)}) copy-start(f32[64]{0:T(128)S(1)} %fusion.195) | copy-start | bytes 772
  327.3 220.8 %copy-start.43 = (f32[4352]{0:T(1024)}, f32[4352]{0:T(1024)S(1)}, u32[]{:S(2)}) copy-start(f32[4352]{0:T(1024)S(1)} %get-tuple-element.393) | copy-start | bytes 52228
  327.3 220.8 %copy-start.45 = (f32[4352]{0:T(1024)}, f32[4352]{0:T(1024)S(1)}, u32[]{:S(2)}) copy-start(f32[4352]{0:T(1024)S(1)} %get-tuple-element.394) | copy-start | bytes 52228
  327.3 220.8 %copy-start.47 = (f32[4352]{0:T(1024)}, f32[4352]{0:T(1024)S(1)}, u32[]{:S(2)}) copy-start(f32[4352]{0:T(1024)S(1)} %get-tuple-element.395) | copy-start | bytes 52228
  833.4 198.8 %all-gather.46.cloned.1.call-start = ((), (), s32[]{:S(2)}) async-start(), calls=%async_computation.7 | async-start | bytes 18874368 | tf_op jit(solution)/shard_map/all_gather | solution.py:117
  849.5 192.8 %all-gather.52.cloned.1.call-start = ((), (), s32[]{:S(2)}) async-start(), calls=%async_computation.10 | async-start | bytes 9437184 | tf_op jit(solution)/shard_map/all_gather | solution.py:118
  850.2 277.8 %all-gather.50.cloned.1.call-start = ((), (), s32[]{:S(2)}) async-start(), calls=%async_computation.9 | async-start | bytes 18874368 | tf_op jit(solution)/shard_map/all_gather | solution.py:117
  851.0 333.2 %all-gather.42.cloned.1.call-start = ((), (), s32[]{:S(2)}) async-start(), calls=%async_computation.5 | async-start | bytes 9437184 | tf_op jit(solution)/shard_map/all_gather | solution.py:115
  851.6 503.2 %all-gather.44.cloned.1.call-start = ((), (), s32[]{:S(2)}) async-start(), calls=%async_computation.6 | async-start | bytes 39518208 | tf_op jit(solution)/shard_map/all_gather | solution.py:116
  852.3 559.2 %all-gather.38.cloned.1.call-start = ((), (), s32[]{:S(2)}) async-start(), calls=%async_computation.3 | async-start | bytes 9437184 | tf_op jit(solution)/shard_map/all_gather | solution.py:115
  852.9 729.8 %all-gather.40.cloned.1.call-start = ((), (), s32[]{:S(2)}) async-start(), calls=%async_computation.4 | async-start | bytes 39518208 | tf_op jit(solution)/shard_map/all_gather | solution.py:116
  992.4 640.8 %reduce-scatter.7.cloned.1.call-start = ((), (), s32[]{:S(2)}) async-start(), calls=%async_computation.17 | async-start | bytes 1253376
  994.2 667.8 %reduce-scatter.9.cloned.1.call-start = ((), (), s32[]{:S(2)}) async-start(), calls=%async_computation.18 | async-start | bytes 1253376
  1014.1 704.1 %all-gather.64.cloned.1.call-start = ((), (), s32[]{:S(2)}) async-start(), calls=%async_computation.16 | async-start | bytes 9437184 | tf_op jit(solution)/shard_map/all_gather | solution.py:257
  1019.0 755.3 %all-gather.62.cloned.1.call-start = ((), (), s32[]{:S(2)}) async-start(), calls=%async_computation.15 | async-start | bytes 9437184 | tf_op jit(solution)/shard_map/all_gather | solution.py:256
  1032.1 1184.9 %all-reduce.60.cloned.1.call-start = ((), (), s32[]{:S(2)}) async-start(), calls=%async_computation.19 | async-start | bytes 25821184 | tf_op jit(solution)/shard_map/psum | solution.py:161
  (122 other events, 2413.7 us)
Sparse Core Ops, SparseCore 0:
  9.9 57.2 all-gather.35
  69.7 183.4 all-gather.53
  255.1 89.8 all-gather.55
  346.8 174.4 all-gather.57
  523.0 89.8 all-gather.59
  833.5 54.0 all-gather.47
  889.5 89.8 all-gather.45
  981.8 54.3 all-gather.51
  1038.2 89.8 all-gather.49
  1129.8 54.3 all-gather.41
  1186.1 168.6 all-gather.43
  1357.1 54.3 all-gather.37
  1414.0 168.6 all-gather.39
  1585.7 36.5 reduce-scatter.6
  1625.4 36.6 reduce-scatter.8
  1663.8 54.3 all-gather.63
  1719.9 54.3 all-gather.61
  1778.2 438.7 all-reduce.59
where the time goes:
time: 2250 us; the launch traced here: 2240 us
  waiting for transfers between devices  1130 us (50%)
  matrix products  451 us (20%)
  local copies, waits for them, and re-layouts  298 us (13%)
  other arithmetic  189 us (8%)
  blocking collectives  145 us (6%)
  between operations  23.9 us (1%)
    psum x1, waiting for transfers between devices, reduce_grads(): lax.psum(parted[1].astype(jnp.bfloat16), 'rep').astype(jnp.float32)  440 us
    all_gather x2, waiting for transfers between devices, reduce_grads(): proj_piece = lax.all_gather(grad_proj, 'shard', axis=0, tiled=True)  342 us
    dot_general x8, matrix products, block_step(): intra = jnp.einsum('tsh,shp->thp', weights, inputs_b, precision=HIGH)  181 us
    slice x2, local copies, waits for them, and re-layouts, mixer(): convolved = conv_bias + padded[0:rows] * conv_weight[0]  180 us
    all_gather x2, waiting for transfers between devices, reduce_grads(): gnorm_piece = lax.all_gather(gnorm, 'shard', axis=0, tiled=True)  85.8 us
    all_gather x2, waiting for transfers between devices, reduce_grads(): normed_piece = lax.all_gather(normed, 'shard', axis=0, tiled=True)  82.2 us
    all_gather x2, waiting for transfers between devices, fetch_forward(): lax.all_gather(pieces[1], 'shard', axis=0, tiled=True)  60.3 us
    all_gather x1, waiting for transfers between devices, body(): lax.all_gather(output_slot, 'shard', axis=0, tiled=True)  53.9 us
  transfers between devices with their start and end apart: 18, of which 10 were waited for; matrix products, arithmetic and copies ran while one was open for 32% of the time, Pallas kernels for 0%

commit v1 on v0

v1 whole, which is shorter than its diff:
```python
import functools

import jax
import jax.numpy as jnp
from jax import lax
from jax.experimental import pallas as pl
from jax.experimental.pallas import tpu as pltpu
from jax.sharding import PartitionSpec as P

LAYERS = 2
EPS = 1e-05
HALF = 128
HEADDIM = 64
GROUP = 256
HPG = GROUP // HEADDIM
STATE = 128
NBC = 3 * STATE
STEPS = 16
LOG2E = 1.4426950408889634
HIGH = lax.Precision.HIGHEST
BF = jnp.bfloat16
F32 = jnp.float32


def nn(a, b, precision=None):
    return lax.dot_general(a, b, (((1,), (0,)), ((), ())), precision=precision, preferred_element_type=F32)


def nt(a, b, precision=None):
    return lax.dot_general(a, b, (((1,), (1,)), ((), ())), precision=precision, preferred_element_type=F32)


def tn(a, b, precision=None):
    return lax.dot_general(a, b, (((0,), (0,)), ((), ())), precision=precision, preferred_element_type=F32)


def sigm(v):
    return 0.5 * jnp.tanh(0.5 * v) + 0.5


def step_parts(v):
    u = jnp.exp(-jnp.abs(v))
    series = u * (1.0 - u * (0.5 - u * (1.0 / 3.0 - u * 0.25)))
    delta = jnp.maximum(v, 0.0) + jnp.where(u < 0.01, series, jnp.log(1.0 + u))
    inv = 1.0 / (1.0 + u)
    sig = jnp.where(v >= 0.0, inv, u * inv)
    safe = jnp.maximum(delta, 1e-30)
    logd = jnp.where(v < -15.0, v, jnp.log(safe))
    rho = jnp.where(v < -15.0, 1.0, sig / safe)
    return delta, sig, logd, rho


def iotas():
    row = lax.broadcasted_iota(jnp.int32, (HALF, HALF), 0)
    col = lax.broadcasted_iota(jnp.int32, (HALF, HALF), 1)
    return row, col


def conv_of(ext, weights, bias):
    out = bias + weights[0:1] * ext[5 : 5 + HALF, :]
    for tap in range(1, 4):
        out = out + weights[tap : tap + 1] * ext[5 + tap : 5 + tap + HALF, :]
    return out


def where_am_i():
    rep = lax.axis_index("rep")
    me = lax.axis_index("shard")
    return rep, me, me // 2, lax.rem(me, 2)


def chip_peer(k):
    rep, _, chip, core = where_am_i()
    return (rep, 2 * jnp.bitwise_xor(chip, k) + core)


def core_peer():
    rep, me, _, _ = where_am_i()
    return (rep, jnp.bitwise_xor(me, 1))


def greet(devices):
    barrier = pltpu.get_barrier_semaphore()
    for device in devices:
        pl.semaphore_signal(barrier, inc=1, device_id=device, device_id_type=pl.DeviceIdType.MESH)
    pl.semaphore_wait(barrier, len(devices))


def push(src, dst, sems, i, device):
    return pltpu.make_async_remote_copy(
        src_ref=src,
        dst_ref=dst,
        send_sem=sems.at[0, i],
        recv_sem=sems.at[1, i],
        device_id=device,
        device_id_type=pl.DeviceIdType.MESH,
    )


def relative(k, side):
    _, _, chip, core = where_am_i()
    return 2 * jnp.bitwise_xor(chip, k) + jnp.bitwise_xor(core, side)


def decay_parts(raw, pbc, lower):
    v = raw + pbc[4:5, 2 * STATE :]
    delta, sig, logd, rho = step_parts(v)
    cum = nn(lower, (LOG2E * pbc[5:6, 2 * STATE :]) * delta, HIGH)
    return delta, sig, rho, cum, cum - LOG2E * logd


def lanes_of(columns, rows):
    lane = lax.broadcasted_iota(jnp.int32, (rows, 128), 1)
    out = jnp.zeros((rows, 128), F32)
    for i, column in enumerate(columns):
        high = column.astype(BF).astype(F32)
        out = jnp.where(lane == 2 * i, high, jnp.where(lane == 2 * i + 1, column - high, out))
    return out.astype(BF)


def load_steps(blocks, wbc, wbc_s, steps):
    count = wbc[0].shape[0]
    part = wbc[0].shape[2]
    wbc_s[2 * STATE + STEPS :, :] = jnp.zeros_like(wbc_s[2 * STATE + STEPS :, :])
    for k in range(count):
        cols = slice(k * part, (k + 1) * part)
        wbc_s[0:STATE, cols] = wbc[0][k]
        wbc_s[STATE : 2 * STATE, cols] = wbc[1][k]
        rows = wbc[2][k]
        if steps < STEPS:
            _, _, chip, _ = where_am_i()
            shift = STEPS - lax.rem(chip * steps, STEPS)
            rows = pltpu.roll(rows.astype(F32), shift, 0)
            live = lax.broadcasted_iota(jnp.int32, rows.shape, 0) < steps
            rows = jnp.where(live, rows, 0.0).astype(BF)
        wbc_s[2 * STATE : 2 * STATE + STEPS, cols] = rows


def load_main(wz, wx, wm_s):
    for k in range(wz.shape[0]):
        cols = slice(k * wz.shape[2], (k + 1) * wz.shape[2])
        wm_s[0:GROUP, cols] = wz[k]
        wm_s[GROUP : 2 * GROUP, cols] = wx[k]


def fwd_kernel(nseq, ng, second, ins, outs, scratch):
    x_refs, refs = ins[:nseq], ins[nseq:]
    wz, wx, wb0, wb1, wdt, wo, pm, pbc = refs[:8]
    if second:
        st_in, hist_m, hist_bc = refs[8:]
    parts, xall, projz, projx, projbc, mixed = outs[:6]
    if not second:
        st_out = outs[6]
    acc, ext, b_s, c_s, s_s, cum_s, rt_s, tail_s, q_s, sq_s, wm_s, wbc_s = scratch
    width = acc.shape[1]
    part = width // (2 * nseq)
    g = pl.program_id(0)
    row, col = iotas()
    tri = row >= col
    left = col < HEADDIM

    @pl.when(g == 0)
    def _():
        for side in range(2):
            for k in range(nseq):
                at = pl.multiple_of(relative(k, side) * part, part)
                to = (side * nseq + k) * part
                for i in range(nseq):
                    xall[i * HALF : (i + 1) * HALF, to : to + part] = x_refs[i][:, pl.ds(at, part)]
        acc[...] = jnp.zeros_like(acc)
        sq_s[...] = jnp.zeros_like(sq_s)
        load_steps(2 * nseq, (wb0, wb1, wdt), wbc_s, ng * HPG)
        projbc[...] = nt(xall[...], wbc_s[...]).reshape(nseq, HALF, NBC)
        lower = jnp.where(tri, 1.0, 0.0)

        def one(s, carry):
            here = projbc[s]
            if second:
                ext[0:8, :] = hist_bc[s, :, : 2 * STATE]
            else:
                ext[0:8, :] = jnp.zeros((8, GROUP), F32)
            ext[8 : 8 + HALF, :] = here[:, : 2 * STATE]
            pre = conv_of(ext, pbc[0:4, : 2 * STATE], pbc[4:5, : 2 * STATE])
            act = pre * sigm(pre)
            keys = act[:, :STATE].astype(BF)
            queries = act[:, STATE:].astype(BF)
            b_s[s] = keys
            c_s[s] = queries
            s_s[s] = nt(queries, keys)
            _, _, _, cum, less = decay_parts(here[:, 2 * STATE :], pbc, lower)
            lesst = less.T
            for gg in range(ng):
                rt_s[gg, s, 0:HPG, :] = lesst[HPG * gg : HPG * (gg + 1), :]
                cum_s[gg, s] = cum if gg == 0 else pltpu.roll(cum, STATE - HPG * gg, 1)
            if not second:
                tail = jnp.exp2(cum[HALF - 1 : HALF, :] - less)
                for gg in range(ng):
                    tail_s[gg, s] = tail if gg == 0 else pltpu.roll(tail, STATE - HPG * gg, 1)
            return carry

        lax.fori_loop(0, nseq, one, 0)

    load_main(wz, wx, wm_s)
    proj = nt(xall[...], wm_s[...])
    projz[...] = proj[:, :GROUP].reshape(nseq, HALF, GROUP)
    projx[...] = proj[:, GROUP:].reshape(nseq, HALF, GROUP)
    params = pm[0]

    def group(s, carry):
        z = projz[s]
        if second:
            ext[0:8, :] = hist_m[s]
        else:
            ext[0:8, :] = jnp.zeros((8, GROUP), F32)
        ext[8 : 8 + HALF, :] = projx[s]
        pre = conv_of(ext, params[0:4], params[4:5])
        xs = pre * sigm(pre)
        xb = xs.astype(BF)
        scores = s_s[s]
        cg = cum_s[g, s]
        rt = rt_s[g, s]
        ys = []
        for pair in range(HPG // 2):
            lanes = slice(pair * 128, (pair + 1) * 128)
            ws, cols = [], []
            for j in (2 * pair, 2 * pair + 1):
                cb = jnp.broadcast_to(cg[:, j : j + 1], (HALF, HALF))
                e = jnp.exp2(jnp.where(tri, cb - rt[j : j + 1, :], -1e30))
                ws.append((e * scores).astype(BF))
                cols.append(cb)
            both = nn(jnp.concatenate(ws, 0), xb[:, lanes])
            y = jnp.where(left, both[:HALF], both[HALF:])
            if second:
                inter = nt(c_s[s], st_in[s, lanes, :].astype(BF))
                y = y + inter * jnp.exp2(jnp.where(left, cols[0], cols[1]))
            else:
                tg = tail_s[g, s]
                tb = jnp.where(left, tg[:, 2 * pair : 2 * pair + 1], tg[:, 2 * pair + 1 : 2 * pair + 2])
                st_out[s, lanes, :] = tn((xs[:, lanes] * tb).astype(BF), b_s[s])
            ys.append(y)
        mix = jnp.concatenate(ys, 1) + params[5:6] * xs
        mixed[s] = mix
        gated = mix * (z * sigm(z))
        here = pl.ds(pl.multiple_of(s * HALF, HALF), HALF)
        q_s[here, :] = (gated * params[6:7]).astype(BF)
        square = gated * gated
        sq_s[here, :] += square[:, :128] + square[:, 128:]
        return carry

    lax.fori_loop(0, nseq, group, 0)
    acc[...] += nn(q_s[...], wo[...])

    @pl.when(g == ng - 1)
    def _():
        for k in range(nseq):
            rows = slice(k * HALF, (k + 1) * HALF)
            parts[k, :, :width] = acc[rows, :].astype(BF)
            parts[k, :, width:] = lanes_of([jnp.sum(sq_s[rows, :], axis=1, keepdims=True)], HALF)


def bwd_kernel(nseq, ng, second, ins, outs, scratch):
    g_refs, t_refs, refs = ins[:nseq], ins[nseq : 2 * nseq], ins[2 * nseq :]
    wz, wx, wb0, wb1, wdt, wo, pm, pbc, projz, projx, projbc, mixed = refs[:12]
    refs = refs[12:]
    if second:
        st_in, hist_m, hist_bc = refs[:3]
    else:
        dst_in, head_m, head_bc = refs[:3]
    parts, gall, gpz, gpx, gpbc, gnorm, sgm, sgbc = outs[:8]
    if second:
        dst_out, hout_m, hout_bc = outs[8:]
    acc, ext, dext, b_s, c_s, s_s, ds_s, db_s, dc_s, cum_s, rt_s, tail_s, dq_s, plus_s, minus_s, csum_s, wm_s, wbc_s, r_b, s_b = scratch
    width = acc.shape[1]
    part = width // (2 * nseq)
    g = pl.program_id(0)
    row, col = iotas()
    tri = row >= col
    left = col < HEADDIM
    lower = jnp.where(tri, 1.0, 0.0)

    def load_bc(s):
        if second:
            ext[0:8, :] = hist_bc[s, :, : 2 * STATE]
        else:
            ext[0:8, :] = jnp.zeros((8, GROUP), F32)
        ext[8 : 8 + HALF, :] = projbc[s, :, : 2 * STATE]
        return conv_of(ext, pbc[0:4, : 2 * STATE], pbc[4:5, : 2 * STATE])

    @pl.when(g == 0)
    def _():
        for k in range(nseq):
            rows = slice(k * HALF, (k + 1) * HALF)
            gall[rows, :] = g_refs[k][...]
            scal = t_refs[k][...].astype(F32)
            r_b[rows, :] = jnp.broadcast_to(scal[:, 0:1] + scal[:, 1:2], (HALF, HALF))
            s_b[rows, :] = jnp.broadcast_to(scal[:, 2:3] + scal[:, 3:4], (HALF, HALF))
        acc[...] = jnp.zeros_like(acc)
        ds_s[...] = jnp.zeros_like(ds_s)
        db_s[...] = jnp.zeros_like(db_s)
        dc_s[...] = jnp.zeros_like(dc_s)
        plus_s[...] = jnp.zeros_like(plus_s)
        minus_s[...] = jnp.zeros_like(minus_s)
        csum_s[...] = jnp.zeros_like(csum_s)
        load_steps(2 * nseq, (wb0, wb1, wdt), wbc_s, ng * HPG)

        def one(s, carry):
            pre = load_bc(s)
            act = pre * sigm(pre)
            keys = act[:, :STATE].astype(BF)
            queries = act[:, STATE:].astype(BF)
            b_s[s] = keys
            c_s[s] = queries
            s_s[s] = nt(queries, keys)
            _, _, _, cum, less = decay_parts(projbc[s, :, 2 * STATE :], pbc, lower)
            lesst = less.T
            for gg in range(ng):
                rt_s[gg, s, 0:HPG, :] = lesst[HPG * gg : HPG * (gg + 1), :]
                cum_s[gg, s] = cum if gg == 0 else pltpu.roll(cum, STATE - HPG * gg, 1)
            if not second:
                tail = jnp.exp2(cum[HALF - 1 : HALF, :] - less)
                for gg in range(ng):
                    tail_s[gg, s] = tail if gg == 0 else pltpu.roll(tail, STATE - HPG * gg, 1)
            return carry

        lax.fori_loop(0, nseq, one, 0)

    dq_s[...] = nt(gall[...], wo[...])
    params = pm[0]
    sgm[...] = jnp.zeros_like(sgm)

    def group(s, carry):
        here = pl.ds(pl.multiple_of(s * HALF, HALF), HALF)
        if second:
            ext[0:8, :] = hist_m[s]
        else:
            ext[0:8, :] = jnp.zeros((8, GROUP), F32)
        ext[8 : 8 + HALF, :] = projx[s]
        pre = conv_of(ext, params[0:4], params[4:5])
        psig = sigm(pre)
        xs = pre * psig
        xb = xs.astype(BF)
        z = projz[s]
        mix = mixed[s]
        sig = sigm(z)
        zs = z * sig
        gated = mix * zs
        rr = r_b[here, :]
        ss = s_b[here, :]
        rr = jnp.concatenate([rr, rr], 1)
        ss = jnp.concatenate([ss, ss], 1)
        dqr = dq_s[here, :] * rr
        gnorm[s] = (gated * rr * params[6:7]).astype(BF)
        sgm[0, 6:7, :] += jnp.sum(dqr * gated, axis=0, keepdims=True)
        dgated = dqr * params[6:7] - ss * gated
        gpz[s] = (dgated * mix * (sig + zs * (1.0 - sig))).astype(BF)
        dmix = dgated * zs
        sgm[0, 5:6, :] += jnp.sum(dmix * xs, axis=0, keepdims=True)
        scores = s_s[s]
        cg = cum_s[g, s]
        rt = rt_s[g, s]
        dmb = dmix.astype(BF)
        dscore = ds_s[s]
        plus = plus_s[s]
        minus = minus_s[s]
        csum = []
        dxs = []
        for pair in range(HPG // 2):
            lanes = slice(pair * 128, (pair + 1) * 128)
            dm = dmix[:, lanes]
            db = dmb[:, lanes]
            zero = jnp.zeros_like(db)
            stack = jnp.concatenate([jnp.where(left, db, zero), jnp.where(left, zero, db)], 0)
            dws = nt(stack, xb[:, lanes])
            cbs = [jnp.broadcast_to(cg[:, j : j + 1], (HALF, HALF)) for j in (2 * pair, 2 * pair + 1)]
            if second:
                edge = jnp.exp2(jnp.where(left, cbs[0], cbs[1]))
                state = st_in[s, lanes, :].astype(BF)
                dye = dm * edge
                dyeb = dye.astype(BF)
                inner = dye * nt(c_s[s], state)
                dc_s[s] += nn(dyeb, state)
                dst_out[s, lanes, :] = tn(dyeb, c_s[s])
            else:
                tg = tail_s[g, s]
                tb = jnp.where(left, tg[:, 2 * pair : 2 * pair + 1], tg[:, 2 * pair + 1 : 2 * pair + 2])
                xst = xs[:, lanes] * tb
                dstate = dst_in[s, lanes, :].astype(BF)
                bds = nt(b_s[s], dstate)
                db_s[s] += nn(xst.astype(BF), dstate)
                inner = xst * bds
            ws = []
            for i, j in enumerate((2 * pair, 2 * pair + 1)):
                e = jnp.exp2(jnp.where(tri, cbs[i] - rt[j : j + 1, :], -1e30))
                ws.append((e * scores).astype(BF))
                t = dws[i * HALF : (i + 1) * HALF] * e
                dscore = dscore + t
                m = t * scores
                csum.append(jnp.sum(m, axis=0, keepdims=True))
                mine = left if i == 0 else jnp.logical_not(left)
                extra = jnp.where(mine, inner, 0.0)
                lane = col == HPG * g + j
                if second:
                    total = jnp.sum(m + extra, axis=1, keepdims=True)
                    plus = jnp.where(lane, total, plus)
                else:
                    plus = jnp.where(lane, jnp.sum(m, axis=1, keepdims=True), plus)
                    minus = jnp.where(lane, jnp.sum(extra, axis=1, keepdims=True), minus)
            dx = params[5:6, lanes] * dm + tn(jnp.concatenate(ws, 0), stack)
            if not second:
                dx = dx + tb * bds
            dxs.append(dx)
        ds_s[s] = dscore
        plus_s[s] = plus
        minus_s[s] = minus
        for j in range(HPG):
            csum_s[g, s, j : j + 1, :] = csum[j]
        dpre = jnp.concatenate(dxs, 1) * (psig + xs * (1.0 - psig))
        sgm[0, 4:5, :] += jnp.sum(dpre, axis=0, keepdims=True)
        dext[0:HALF, :] = dpre
        if second:
            dext[HALF : HALF + 8, :] = jnp.zeros((8, GROUP), F32)
            hout_m[s] = dpre[0:8, :]
        else:
            dext[HALF : HALF + 8, :] = head_m[s]
        dcin = jnp.zeros((HALF, GROUP), F32)
        for tap in range(4):
            sgm[0, tap : tap + 1, :] += jnp.sum(dpre * ext[5 + tap : 5 + tap + HALF, :], axis=0, keepdims=True)
            dcin = dcin + params[tap : tap + 1] * dext[3 - tap : 3 - tap + HALF, :]
        gpx[s] = dcin.astype(BF)
        return carry

    lax.fori_loop(0, nseq, group, 0)
    gz = gpz[...].reshape(nseq * HALF, GROUP)
    gx = gpx[...].reshape(nseq * HALF, GROUP)
    load_main(wz, wx, wm_s)
    acc[...] += nn(jnp.concatenate([gz, gx], 1), wm_s[...])

    @pl.when(g == ng - 1)
    def _():
        sgbc[...] = jnp.zeros_like(sgbc)
        upper = jnp.where(row <= col, 1.0, 0.0)

        def one(s, carry):
            pre = load_bc(s)
            psig = sigm(pre)
            act = pre * psig
            dsb = ds_s[s].astype(BF)
            dkeys = db_s[s] + tn(dsb, c_s[s])
            dqueries = dc_s[s] + nn(dsb, b_s[s])
            dpre = jnp.concatenate([dkeys, dqueries], 1) * (psig + act * (1.0 - psig))
            sgbc[4:5, : 2 * STATE] += jnp.sum(dpre, axis=0, keepdims=True)
            dext[0:HALF, :] = dpre
            if second:
                dext[HALF : HALF + 8, :] = jnp.zeros((8, GROUP), F32)
                hout_bc[s] = dpre[0:8, :]
            else:
                dext[HALF : HALF + 8, :] = head_bc[s]
            dcin = jnp.zeros((HALF, GROUP), F32)
            for tap in range(4):
                sgbc[tap : tap + 1, : 2 * STATE] += jnp.sum(
                    dpre * ext[5 + tap : 5 + tap + HALF, :], axis=0, keepdims=True
                )
                dcin = dcin + pbc[tap : tap + 1, : 2 * STATE] * dext[3 - tap : 3 - tap + HALF, :]
            gpbc[s, :, : 2 * STATE] = dcin.astype(BF)
            delta, sig, rho, _, _ = decay_parts(projbc[s, :, 2 * STATE :], pbc, lower)
            rate = pbc[5:6, 2 * STATE :]
            minus = minus_s[s]
            sums = [csum_s[gg, s, 0:HPG, :] for gg in range(ng)]
            sums = jnp.concatenate(sums + [jnp.zeros((STATE - ng * HPG, HALF), F32)], 0)
            direct = sums.T + minus
            last = jnp.where(row == HALF - 1, jnp.sum(minus, axis=0, keepdims=True), 0.0)
            dlog = nn(upper, plus_s[s] - direct + last, HIGH)
            sgbc[5:6, 2 * STATE :] += jnp.sum(dlog * rate * delta, axis=0, keepdims=True)
            dv = dlog * rate * sig + direct * rho
            sgbc[4:5, 2 * STATE :] += jnp.sum(dv, axis=0, keepdims=True)
            gpbc[s, :, 2 * STATE :] = dv.astype(BF)
            return carry

        lax.fori_loop(0, nseq, one, 0)
        gb = gpbc[...].reshape(nseq * HALF, NBC)
        acc[...] += nn(gb, wbc_s[...])
        for side in range(2):
            for k in range(nseq):
                to = pl.multiple_of(relative(k, side) * part, part)
                at = (side * nseq + k) * part
                for i in range(nseq):
                    parts[i, :, pl.ds(to, part)] = acc[i * HALF : (i + 1) * HALF, at : at + part].astype(BF)


ANY = pl.BlockSpec(memory_space=pl.ANY)


def whole(shape):
    return pl.BlockSpec(shape, lambda g: (0,) * len(shape))


def row_of(array, k, lanes=None, lane_block=0):
    lanes = array.shape[2] if lanes is None else lanes
    return (array, pl.BlockSpec((None, array.shape[1], lanes), lambda g: (k, 0, lane_block)))


def full(array):
    return (array, whole(array.shape))


def struct(shape, dtype):
    return jax.ShapeDtypeStruct(tuple(shape), dtype)


def vm(shape, dtype):
    return (struct(shape, dtype), whole(tuple(shape)))


def on_line(count):
    rep, me, _, _ = where_am_i()
    low = rep < count // 2
    depth = jnp.where(low, rep, count - 1 - rep)
    inner = jnp.where(low, rep + 1, rep - 1)
    outer = jnp.where(depth == 0, count - 1 - rep, jnp.where(low, rep - 1, rep + 1))
    return depth, (inner, me), (outer, me)


def peer_device(peer):
    rep, me, _, _ = where_am_i()
    if peer == "core":
        return core_peer()
    if peer == "pair":
        return (rep + 1 - 2 * lax.rem(rep, 2), me)
    if peer in ("inner", "outer"):
        _, inner, outer = on_line(lax.axis_size("rep"))
        return inner if peer == "inner" else outer
    return chip_peer(peer)


class Task:
    def __init__(self, ins, outs, scratch, start, finish, peers=()):
        self.ins, self.outs, self.scratch = ins, outs, scratch
        self.start, self.finish, self.peers = start, finish, peers


def launch(name, cid, steps, main, ins, outs, scratch, tasks, flops=0, limit=62):
    groups = [(ins, outs, scratch)] + [(task.ins, task.outs, task.scratch) for task in tasks]
    all_ins = sum((list(group[0]) for group in groups), [])
    all_outs = sum((list(group[1]) for group in groups), [])
    all_scratch = sum((list(group[2]) for group in groups), [])
    peers = []
    for task in tasks:
        for peer in task.peers:
            if peer not in peers:
                peers.append(peer)

    def split(refs, which):
        parts, at = [], 0
        for group in groups:
            count = len(group[which])
            parts.append(refs[at : at + count])
            at += count
        return parts

    def kernel(*refs):
        refs = list(refs)
        a, b = len(all_ins), len(all_ins) + len(all_outs)
        parts = list(zip(split(refs[:a], 0), split(refs[a:b], 1), split(refs[b:], 2)))
        g = pl.program_id(0)

        @pl.when(g == 0)
        def _():
            if peers:
                greet([peer_device(peer) for peer in peers])
            for task, part in zip(tasks, parts[1:]):
                task.start(*part)

        if main is not None:
            main(*parts[0])

        @pl.when(g == steps - 1)
        def _():
            for task, part in reversed(list(zip(tasks, parts[1:]))):
                task.finish(*part)

    params = dict(vmem_limit_bytes=limit << 20)
    if peers:
        params.update(collective_id=cid, has_side_effects=True)
    res = pl.pallas_call(
        kernel,
        grid=(steps,),
        in_specs=[spec for _, spec in all_ins],
        out_specs=[spec for _, spec in all_outs],
        out_shape=[shape for shape, _ in all_outs],
        scratch_shapes=all_scratch,
        compiler_params=pltpu.CompilerParams(**params),
        cost_estimate=pl.CostEstimate(flops=flops, bytes_accessed=40 << 20, transcendentals=0),
        name=name,
    )(*[array for array, _ in all_ins])
    return split(list(res), 1)


def gather_task(arrays, nch):
    count = len(arrays)

    def copies(ins, outs, scr):
        return [
            push(ins[i], outs[i].at[k - 1], scr[0], i * nch + k, chip_peer(k)) for k in range(1, nch) for i in range(count)
        ]

    def start(ins, outs, scr):
        for copy in copies(ins, outs, scr):
            copy.start()

    def finish(ins, outs, scr):
        for copy in copies(ins, outs, scr):
            copy.wait()

    return Task(
        [(array, ANY) for array in arrays],
        [(struct((nch - 1,) + array.shape, array.dtype), ANY) for array in arrays],
        [pltpu.SemaphoreType.DMA((2, count * nch))],
        start,
        finish,
        tuple(range(1, nch)),
    )


def collect_task(parts, ins, outs, scratch, work, share):
    nch = parts.shape[0]
    shared = []
    if share:
        last = outs[-1][0]
        shared = [(struct((nch - 1,) + last.shape, last.dtype), ANY)]

    def copies(ins, scr):
        return [push(ins[0].at[k], scr[1].at[k - 1], scr[0], k, chip_peer(k)) for k in range(1, nch)]

    def start(ins, outs, scr):
        for copy in copies(ins, scr):
            copy.start()

    def finish(ins, outs, scr):
        for copy in copies(ins, scr):
            copy.wait()

        def total(rows, cols):
            value = ins[1][rows, cols].astype(F32)
            for k in range(nch - 1):
                value = value + scr[1][k, rows, cols].astype(F32)
            return value

        work(total, ins[2:], outs, scr[2:])
        if share:
            sent = [push(outs[-2], outs[-1].at[k - 1], scr[0], nch + k, chip_peer(k)) for k in range(1, nch)]
            for copy in sent:
                copy.start()
            for copy in sent:
                copy.wait()

    return Task(
        [(parts, ANY), row_of(parts, 0)] + ins,
        outs + shared,
        [pltpu.SemaphoreType.DMA((2, 2 * nch)), pltpu.VMEM((nch - 1,) + parts.shape[1:], BF)] + scratch,
        start,
        finish,
        tuple(range(1, nch)),
    )


def by_rows(body):
    def step(i, carry):
        body(pl.ds(pl.multiple_of(i * 16, 16), 16))
        return carry

    lax.fori_loop(0, HALF // 16, step, 0)


def owner_fwd(parts, stream, mask, gain, gb, inner, share=False):
    width = stream[0].shape[-1]
    last = gain is None

    def work(total, ins, outs, scr):
        def body(rows):
            branch = total(rows, slice(0, width))
            tile = total(rows, slice(width, width + 128))
            scale = lax.rsqrt((tile[:, 0:1] + tile[:, 1:2]) * (1.0 / inner) + EPS)
            branch = branch * scale
            outs[0][rows, :] = branch
            value = ins[0][rows, :] + ins[1][rows, 0:1] * branch
            if last:
                outs[1][rows, :] = value.astype(BF)
                dots = jnp.sum(ins[2][rows, :].astype(F32) * branch, axis=1, keepdims=True)
                outs[2][rows, :] = lanes_of([scale, scale * scale * dots * (1.0 / inner)], 16)
            else:
                outs[1][rows, :] = value
                inv = lax.rsqrt(jnp.mean(value * value, axis=1, keepdims=True) + EPS)
                outs[2][rows, :] = (value * inv * ins[2][0:1, :]).astype(BF)
                outs[3][rows, :] = jnp.broadcast_to(scale, (16, 128))

        by_rows(body)

    shape = (HALF, width)
    outs = [vm(shape, F32), vm(shape, BF if last else F32)]
    outs += [vm((HALF, 128), BF)] if last else [vm(shape, BF), vm((HALF, 128), F32)]
    return collect_task(parts, [stream, full(mask), gb if last else gain], outs, [], work, share)


def owner_bwd(parts, stream, gain, flow, mask, branch, scale, inner):
    width = stream[0].shape[-1]
    first = branch is None

    def work(total, ins, outs, scr):
        outs[0][...] = jnp.zeros_like(outs[0])

        def body(rows):
            gx = total(rows, slice(0, width))
            value = ins[0][rows, :]
            inv = lax.rsqrt(jnp.mean(value * value, axis=1, keepdims=True) + EPS)
            outs[0][0:1, :] += jnp.sum(gx * value * inv, axis=0, keepdims=True)
            gs = gx * ins[1][0:1, :]
            coef = inv * inv * inv * jnp.mean(gs * value, axis=1, keepdims=True)
            new = ins[2][rows, :].astype(F32) + inv * gs - value * coef
            if first:
                outs[1][rows, :] = new.astype(BF)
            else:
                outs[1][rows, :] = new
                gb = (ins[3][rows, 0:1] * new).astype(BF)
                dots = jnp.sum(gb.astype(F32) * ins[4][rows, :], axis=1, keepdims=True)
                rate = ins[5][rows, 0:1]
                outs[2][rows, :width] = gb
                outs[2][rows, width:] = lanes_of([rate, rate * rate * dots * (1.0 / inner)], 16)

        by_rows(body)

    shape = (HALF, width)
    outs = [vm((8, width), F32), vm(shape, BF if first else F32)]
    ins = [stream, gain, flow]
    if not first:
        outs.append(vm((HALF, width + 128), BF))
        ins += [full(mask), full(branch), full(scale)]
    return collect_task(parts, ins, outs, [], work, False)


def group_out(nseq, inner, dtype):
    return (struct((nseq, HALF, inner), dtype), pl.BlockSpec((nseq, HALF, GROUP), lambda g: (0, 0, g)))


def weight_ins(w, wo, pm, pbc, layer):
    _, count, tall, part = w.shape
    width = wo.shape[1]
    at = (tall - STATE - STEPS) // STATE

    def rows(which, height, block):
        return (w, pl.BlockSpec((None, count, height, part), lambda g: (which, 0, block if block is not None else g, 0)))

    return [
        rows(0, GROUP, None),
        rows(1, GROUP, None),
        rows(0, STATE, at),
        rows(1, STATE, at),
        rows(0, STEPS, (tall - STEPS) // STEPS),
        (wo, pl.BlockSpec((GROUP, width), lambda g: (g, 0))),
        (pm, pl.BlockSpec((None, 1, 16, GROUP), lambda g: (layer, g, 0, 0))),
        (pbc, pl.BlockSpec((None, 8, NBC), lambda g: (layer, 0, 0))),
    ]


def grouped(array):
    count, rows, _ = array.shape
    return (array, pl.BlockSpec((count, rows, GROUP), lambda g: (0, 0, g)))


def grouped_tail(array):
    return (array, pl.BlockSpec((array.shape[0], 8, GROUP), lambda g: (0, HALF // 8 - 1, g)))


def state_of(array):
    return (array, pl.BlockSpec((array.shape[0], GROUP, STATE), lambda g: (0, g, 0)))


def bc_tail(array):
    return (array, pl.BlockSpec((array.shape[0], 8, NBC), lambda g: (0, HALF // 8 - 1, 0)))


def run_fwd(cid, xs, weights, previous, tasks):
    nseq = len(xs)
    wo = weights[5][0]
    inner, width = wo.shape
    ng = inner // GROUP
    rows = nseq * HALF
    second = previous is not None
    ins = list(xs) + list(weights)
    if second:
        ins += [state_of(previous["state"]), grouped_tail(previous["projx"]), bc_tail(previous["projbc"])]
    outs = [
        vm((nseq, HALF, width + 128), BF),
        vm((rows, width), BF),
        group_out(nseq, inner, F32),
        group_out(nseq, inner, F32),
        vm((nseq, HALF, NBC), F32),
        group_out(nseq, inner, F32),
    ]
    if not second:
        outs.append((struct((nseq, inner, STATE), F32), pl.BlockSpec((nseq, GROUP, STATE), lambda g: (0, g, 0))))
    scratch = [
        pltpu.VMEM((rows, width), F32),
        pltpu.VMEM((8 + HALF, GROUP), F32),
        pltpu.VMEM((nseq, HALF, STATE), BF),
        pltpu.VMEM((nseq, HALF, STATE), BF),
        pltpu.VMEM((nseq, HALF, HALF), F32),
        pltpu.VMEM((ng, nseq, HALF, STATE), F32),
        pltpu.VMEM((ng, nseq, 8, HALF), F32),
        pltpu.VMEM((ng, nseq, HALF, STATE), F32),
        pltpu.VMEM((rows, GROUP), BF),
        pltpu.VMEM((rows, 128), F32),
        pltpu.VMEM((2 * GROUP, width), BF),
        pltpu.VMEM((NBC, width), BF),
    ]
    name = "fwd_second" if second else "fwd_first"
    main = functools.partial(fwd_kernel, nseq, ng, second)
    res = launch(name, cid, ng, main, ins, outs, scratch, tasks, 4 * rows * width * (3 * inner + NBC))
    keys = ["parts", "xall", "projz", "projx", "projbc", "mixed", "state"]
    out = dict(zip(keys, res[0]))
    if second:
        out["state"] = previous["state"]
    return out, res[1:]


def run_bwd(cid, gs, scals, weights, saved, other, later, tasks):
    nseq = len(gs)
    wo = weights[5][0]
    inner, width = wo.shape
    ng = inner // GROUP
    rows = nseq * HALF
    second = later is None
    ins = list(gs) + list(scals) + list(weights)
    ins += [grouped(saved["projz"]), grouped(saved["projx"]), full(saved["projbc"]), grouped(saved["mixed"])]
    if second:
        ins += [state_of(other["state"]), grouped_tail(other["projx"]), bc_tail(other["projbc"])]
    else:
        ins += [state_of(later["dstate"]), grouped(later["head_m"]), full(later["head_bc"])]
    outs = [
        vm((nseq, HALF, width), BF),
        vm((rows, width), BF),
        group_out(nseq, inner, BF),
        group_out(nseq, inner, BF),
        vm((nseq, HALF, NBC), BF),
        group_out(nseq, inner, BF),
        (struct((ng, 8, GROUP), F32), pl.BlockSpec((1, 8, GROUP), lambda g: (g, 0, 0))),
        vm((8, NBC), F32),
    ]
    if second:
        outs += [
            (struct((nseq, inner, STATE), F32), pl.BlockSpec((nseq, GROUP, STATE), lambda g: (0, g, 0))),
            (struct((nseq, 8, inner), F32), pl.BlockSpec((nseq, 8, GROUP), lambda g: (0, 0, g))),
            vm((nseq, 8, GROUP), F32),
        ]
    square = pltpu.VMEM((nseq, HALF, HALF), F32)
    scratch = [
        pltpu.VMEM((rows, width), F32),
        pltpu.VMEM((8 + HALF, GROUP), F32),
        pltpu.VMEM((8 + HALF, GROUP), F32),
        pltpu.VMEM((nseq, HALF, STATE), BF),
        pltpu.VMEM((nseq, HALF, STATE), BF),
        square,
        square,
        square,
        square,
        pltpu.VMEM((ng, nseq, HALF, STATE), F32),
        pltpu.VMEM((ng, nseq, 8, HALF), F32),
        pltpu.VMEM((ng, nseq, HALF, STATE), F32),
        pltpu.VMEM((rows, GROUP), F32),
        square,
        square,
        pltpu.VMEM((ng, nseq, 8, HALF), F32),
        pltpu.VMEM((2 * GROUP, width), BF),
        pltpu.VMEM((NBC, width), BF),
        pltpu.VMEM((rows, HALF), F32),
        pltpu.VMEM((rows, HALF), F32),
    ]
    name = "bwd_second" if second else "bwd_first"
    main = functools.partial(bwd_kernel, nseq, ng, second)
    res = launch(name, cid, ng, main, ins, outs, scratch, tasks, 8 * rows * width * (3 * inner + NBC))
    keys = ["parts", "gall", "gpz", "gpx", "gpbc", "gnorm", "sgm", "sgbc", "dstate", "head_m", "head_bc"]
    return dict(zip(keys, res[0])), res[1:]


def grads_task(nch, xa, xb, za, zb, ma, mb, ba, bb, qa, qb, ga, gb):
    rows, width = xa.shape
    local = za.shape[1]
    part = width // (2 * nch)
    tall = 2 * local + 2 * STATE + STEPS
    half = local // 2

    quarter = half // 4
    block = 256

    def halves(ins, side, put_in, put_out, before, after):
        xa, xb, za, zb, ma, mb, ba, bb, qa, qb, ga, gb = ins
        _, _, _, core = where_am_i()
        for k in range(nch):
            before(k)
            cols = slice((side * nch + k) * part, (side * nch + k + 1) * part)
            ax, bx = xa[:, cols], xb[:, cols]
            for i, (a, b) in enumerate(((za, zb), (ma, mb))):
                for at in range(0, local, 512):
                    span = slice(at, at + 512)
                    put_in(k, i * local + at, tn(a[:, span], ax) + tn(b[:, span], bx))
            value = tn(ba[...], ax) + tn(bb[...], bx)
            put_in(k, 2 * local, value[: 2 * STATE + STEPS])
            after(k)
        before(nch)
        base = jnp.bitwise_xor(core, side) * half
        for at in range(0, half, block):
            span = pl.ds(pl.multiple_of(base + at, block), block)
            aq, bq = qa[:, span], qb[:, span]
            for lane in range(0, width, 512):
                cols = slice(lane, lane + 512)
                put_out(at, cols, tn(aq, ga[:, cols]) + tn(bq, gb[:, cols]))
        after(nch)

    def nothing(k):
        return None

    def copies(scr, k):
        sems, away_in, away_out, came_in, came_out = scr
        if k == nch:
            return push(away_out, came_out, sems, nch, core_peer())
        return push(away_in.at[k], came_in.at[k], sems, k, core_peer())

    def start(ins, outs, scr):
        _, away_in, away_out, _, _ = scr

        def put_in(k, at, value):
            away_in[k, at : at + value.shape[0], :] = value.astype(BF)

        def put_out(at, cols, value):
            away_out[at : at + block, cols] = value.astype(BF)

        halves(ins, 1, put_in, put_out, nothing, lambda k: copies(scr, k).start())

    def finish(ins, outs, scr):
        _, _, _, came_in, came_out = scr

        def put_in(k, at, value):
            rows = slice(at, at + value.shape[0])
            outs[k][rows, :] = (value + came_in[k, rows, :].astype(F32)).astype(BF)

        def put_out(at, cols, value):
            for row in range(at, at + block, min(quarter, block)):
                i, to = divmod(row, quarter)
                size = min(quarter, block)
                piece = value[row - at : row - at + size] + came_out[row : row + size, cols].astype(F32)
                outs[nch + i][to : to + size, cols] = piece.astype(BF)

        halves(ins, 0, put_in, put_out, lambda k: copies(scr, k).wait(), nothing)

    arrays = [xa, xb, za, zb, ma, mb, ba, bb, qa, qb, ga, gb]
    big, small = (nch, tall, part), (half, width)
    return Task(
        [full(array) for array in arrays],
        [vm((tall, part), BF)] * nch + [vm((quarter, width), BF)] * 4,
        [pltpu.SemaphoreType.DMA((2, nch + 1))]
        + [pltpu.VMEM(big, BF), pltpu.VMEM(small, BF), pltpu.VMEM(big, BF), pltpu.VMEM(small, BF)],
        start,
        finish,
        ("core",),
    )


def pieces_of(to, which, nch, inner, channels):
    local = inner // nch
    steps = local // HEADDIM
    first = pl.multiple_of(which * inner + to * local, GROUP)
    second = pl.multiple_of(2 * inner + which * STATE, STATE)
    third = pl.multiple_of(inner + channels + (to * steps) // STEPS * STEPS, STEPS)
    return [(first, 0, local), (second, local, STATE), (third, local + STATE, STEPS)]


def start_kernel(
    nch, inner, channels, tr, tokens, small, out_proj, w, toks, smalls, wo0, wo1, sems, local_sems, own_w, own_t, own_s, own_o
):
    rep, me, chip, core = where_am_i()
    zpar = lax.rem(rep, 2)
    zdev = (rep + 1 - 2 * zpar, me)
    cdev = core_peer()
    greet([chip_peer(k) for k in range(1, nch)] + [cdev, zdev])
    number = iter(range(1000))
    waits, loads, stores = [], [], []

    def go(src, dst, device):
        copy = push(src, dst, sems, next(number), device)
        copy.start()
        waits.append(copy)
        return copy

    def here(src, stage, dst):
        i = len(loads)
        load = pltpu.make_async_copy(src, stage, local_sems.at[0, i])
        load.start()
        loads.append(load)
        stores.append(pltpu.make_async_copy(stage, dst, local_sems.at[1, i]))

    def rows(ref, at, count):
        return ref.at[pl.ds(at, count), :]

    fetched = []
    for k in range(1, nch):
        to = jnp.bitwise_xor(chip, k)
        fetched.append(
            [
                go(rows(tr.at[0], at, count), rows(w.at[zpar, k], put, count), chip_peer(k))
                for at, put, count in pieces_of(to, zpar, nch, inner, channels)
            ]
        )
    got_small = [go(small, smalls.at[k], chip_peer(k)) for k in range(1, nch)]
    got_first = [go(rows(tokens.at[0], 0, HALF), toks.at[k, pl.ds(0, HALF), :], chip_peer(k)) for k in range(1, nch)]
    for which in range(2):
        for at, put, count in pieces_of(chip, which, nch, inner, channels):
            here(rows(tr.at[0], at, count), rows(own_w.at[which], put, count), rows(w.at[which, 0], put, count))
            go(rows(tr.at[0], at, count), rows(w.at[which, nch], put, count), cdev)
    here(small, own_s, smalls.at[0])
    here(tokens.at[0], own_t, toks.at[0])
    go(small, smalls.at[nch], cdev)
    go(tokens.at[0], toks.at[nch], cdev)
    half = out_proj.shape[1]
    at = pl.multiple_of(core * half, half)
    for layer, wo in enumerate((wo0, wo1)):
        here(out_proj.at[layer], own_o.at[layer], rows(wo, at, half))
        go(out_proj.at[layer], rows(wo, at, half), cdev)
    for load, store in zip(loads, stores):
        load.wait()
        store.start()
    swapped = []
    for k in range(1, nch):
        for copy in fetched[k - 1]:
            copy.wait_recv()
        swapped.append(go(w.at[zpar, k], w.at[zpar, k], zdev))
        go(w.at[zpar, k], w.at[zpar, nch + k], cdev)
    got_last = [
        go(rows(tokens.at[0], HALF, HALF), toks.at[k, pl.ds(HALF, HALF), :], chip_peer(k)) for k in range(1, nch)
    ]
    for k in range(1, nch):
        got_small[k - 1].wait_recv()
        go(smalls.at[k], smalls.at[nch + k], cdev)
        got_first[k - 1].wait_recv()
        go(toks.at[k, pl.ds(0, HALF), :], toks.at[nch + k, pl.ds(0, HALF), :], cdev)
    for k in range(1, nch):
        swapped[k - 1].wait_recv()
        go(w.at[1 - zpar, k], w.at[1 - zpar, nch + k], cdev)
    for k in range(1, nch):
        got_last[k - 1].wait_recv()
        go(toks.at[k, pl.ds(HALF, HALF), :], toks.at[nch + k, pl.ds(HALF, HALF), :], cdev)
    received = set(map(id, sum(fetched, []) + got_small + got_first + got_last + swapped))
    for copy in waits:
        copy.wait_send()
        if id(copy) not in received:
            copy.wait_recv()
    for copy in stores:
        copy.wait()


def start_up(tr, tokens, small, out_proj, nch, inner, channels):
    n = 2 * nch
    local = inner // nch
    part = tr.shape[2]
    width = tokens.shape[2]
    outs = [
        struct((2, n, local + STATE + STEPS, part), BF),
        struct((n,) + tokens.shape[1:], BF),
        struct((n,) + small.shape, BF),
        struct((local, width), BF),
        struct((local, width), BF),
    ]
    return pl.pallas_call(
        functools.partial(start_kernel, nch, inner, channels),
        in_specs=[ANY] * 4,
        out_specs=[ANY] * 5,
        out_shape=outs,
        scratch_shapes=[
            pltpu.SemaphoreType.DMA((2, 16 * nch + 16)),
            pltpu.SemaphoreType.DMA((2, 16)),
            pltpu.VMEM((2, local + STATE + STEPS, part), BF),
            pltpu.VMEM(tokens.shape[1:], BF),
            pltpu.VMEM(small.shape, BF),
            pltpu.VMEM(out_proj.shape, BF),
        ],
        compiler_params=pltpu.CompilerParams(collective_id=1, has_side_effects=True, vmem_limit_bytes=40 << 20),
        name="start_up",
    )(tr, tokens, small, out_proj)


def fetch_task(tr, layer, nch, inner, channels):
    tall = inner // nch + STATE + STEPS

    def copies(ins, outs, scr):
        rep, _, chip, _ = where_am_i()
        zpar = lax.rem(rep, 2)
        out = []
        for k in range(1, nch):
            to = jnp.bitwise_xor(chip, k)
            for i, (at, put, count) in enumerate(pieces_of(to, zpar, nch, inner, channels)):
                src = ins[0].at[layer, pl.ds(at, count), :]
                out.append(push(src, outs[0].at[k - 1, pl.ds(put, count), :], scr[0], 3 * k + i, chip_peer(k)))
        return out

    def start(ins, outs, scr):
        for copy in copies(ins, outs, scr):
            copy.start()

    def finish(ins, outs, scr):
        for copy in copies(ins, outs, scr):
            copy.wait()

    return Task(
        [(tr, ANY)],
        [(struct((nch - 1, tall, tr.shape[2]), BF), ANY)],
        [pltpu.SemaphoreType.DMA((2, 3 * nch))],
        start,
        finish,
        tuple(range(1, nch)),
    )


def finish_task(tr, fetched, layer, nch, inner, channels):
    n = 2 * nch
    tall = inner // nch + STATE + STEPS

    def plan(ins, outs, scr):
        rep, me, chip, core = where_am_i()
        zpar = lax.rem(rep, 2)
        zdev = (rep + 1 - 2 * zpar, me)
        cdev = core_peer()
        source, got, w = ins[0], ins[1], outs[0]
        near, far, here = [], [], []
        for k in range(1, nch):
            near.append(push(got.at[k - 1], w.at[zpar, k], scr[0], k, zdev))
            near.append(push(got.at[k - 1], w.at[zpar, nch + k], scr[0], nch + k, cdev))
            far.append(push(w.at[1 - zpar, k], w.at[1 - zpar, nch + k], scr[0], 2 * nch + k, cdev))
            here.append((got.at[k - 1], scr[2].at[k - 1], w.at[zpar, k]))
        i = 0
        for which in range(2):
            for at, put, count in pieces_of(chip, which, nch, inner, channels):
                src = source.at[layer, pl.ds(at, count), :]
                near.append(push(src, w.at[which, nch, pl.ds(put, count), :], scr[0], 3 * nch + i, cdev))
                stage = scr[2].at[nch - 1 + which, pl.ds(put, count), :]
                here.append((src, stage, w.at[which, 0, pl.ds(put, count), :]))
                i += 1
        loads = [pltpu.make_async_copy(src, stage, scr[1].at[0, i]) for i, (src, stage, _) in enumerate(here)]
        stores = [pltpu.make_async_copy(stage, dst, scr[1].at[1, i]) for i, (_, stage, dst) in enumerate(here)]
        return near, far, loads, stores

    def start(ins, outs, scr):
        near, _, loads, stores = plan(ins, outs, scr)
        for copy in near + loads:
            copy.start()
        for load, store in zip(loads, stores):
            load.wait()
            store.start()

    def finish(ins, outs, scr):
        near, far, _, stores = plan(ins, outs, scr)
        for k in range(1, nch):
            near[2 * (k - 1)].wait_recv()
            far[k - 1].start()
        for copy in stores:
            copy.wait()
        for i, copy in enumerate(near):
            copy.wait_send()
            if i >= 2 * (nch - 1) or i % 2:
                copy.wait_recv()
        for copy in far:
            copy.wait()

    return Task(
        [(tr, ANY), (fetched, ANY)],
        [(struct((2, n, tall, tr.shape[2]), BF), ANY)],
        [
            pltpu.SemaphoreType.DMA((2, 3 * nch + 6)),
            pltpu.SemaphoreType.DMA((2, nch + 6)),
            pltpu.VMEM((nch + 1, tall, tr.shape[2]), BF),
        ],
        start,
        finish,
        tuple(range(1, nch)) + ("core", "pair"),
    )


def params_kernel(nch, n, sizes, index, small, gains, pm, pbc, full_s):
    chip, core = index[0], index[1]
    part, gate_n, conv_n, head_n = sizes
    _, ng, _, _ = pm.shape
    local = ng * GROUP
    steps = 2 * head_n
    at_dt = part + gate_n
    row = lax.broadcasted_iota(jnp.int32, (STATE, local), 0)
    col = lax.broadcasted_iota(jnp.int32, (STATE, local), 1)
    expand = jnp.where(col // HEADDIM == row, 1.0, 0.0).astype(BF)
    lane = lax.broadcasted_iota(jnp.int32, (1, STATE), 1)

    def rel(q):
        return jnp.bitwise_xor(core, q % 2) * nch + jnp.bitwise_xor(chip, q // 2)

    for q in range(n):
        here = small[rel(q)].astype(F32)
        for layer in range(LAYERS):
            gains[layer, :, q * part : (q + 1) * part] = jnp.broadcast_to(here[8 * layer : 8 * layer + 1, :part], (8, part))
            full_s[8 * layer : 8 * layer + 5, q * conv_n : (q + 1) * conv_n] = here[8 * layer + 1 : 8 * layer + 6, :conv_n]
    own = [small[jnp.bitwise_xor(core, c) * nch].astype(F32) for c in range(2)]
    pm[...] = jnp.zeros_like(pm)
    pbc[...] = jnp.zeros_like(pbc)
    for layer in range(LAYERS):
        top = [item[8 * layer : 8 * layer + 1] for item in own]

        def heads(at):
            first = jnp.where(lane < head_n, top[0][:, at : at + STATE], 0.0)
            last = jnp.where(lane < head_n, top[1][:, at : at + STATE], 0.0)
            return first + pltpu.roll(last, head_n, 1)

        skip = nn(jnp.broadcast_to(heads(at_dt + 2 * STATE), (8, STATE)).astype(BF), expand)
        for g in range(ng):
            cols = pl.ds(pl.multiple_of(chip * local + g * GROUP, GROUP), GROUP)
            pm[layer, g, 0:5, :] = full_s[8 * layer : 8 * layer + 5, cols]
            pm[layer, g, 5:6, :] = skip[0:1, g * GROUP : (g + 1) * GROUP]
            which, at = divmod(g * GROUP, gate_n)
            pm[layer, g, 6:7, :] = top[which][:, part + at : part + at + GROUP]
        inner = nch * local
        pbc[layer, 0:5, : 2 * STATE] = full_s[8 * layer : 8 * layer + 5, inner : inner + 2 * STATE]
        pbc[layer, 4:5, 2 * STATE :] = heads(at_dt)
        pbc[layer, 5:6, 2 * STATE :] = jnp.where(lane < steps, -jnp.exp(heads(at_dt + STATE)), 0.0)


def make_params(index, small, nch, ng, sizes):
    n = 2 * nch
    width = small.shape[2]
    part, gate_n, conv_n, head_n = sizes
    shapes = [(LAYERS, 8, width), (LAYERS, ng, 16, GROUP), (LAYERS, 8, NBC)]
    return pl.pallas_call(
        functools.partial(params_kernel, nch, n, sizes),
        grid_spec=pltpu.PrefetchScalarGridSpec(
            num_scalar_prefetch=1,
            grid=(1,),
            in_specs=[pl.BlockSpec(small.shape, lambda i, idx: (0, 0, 0))],
            out_specs=[pl.BlockSpec(shape, lambda i, idx, m=len(shape): (0,) * m) for shape in shapes],
            scratch_shapes=[pltpu.VMEM((16, n * conv_n), F32)],
        ),
        out_shape=[struct(shape, F32) for shape in shapes],
        name="params",
    )(index, small)


def pick_kernel(slots, tok, gain, xs, stream):
    value = tok[...].astype(F32)
    inv = lax.rsqrt(jnp.mean(value * value, axis=1, keepdims=True) + EPS)
    xs[...] = (value * inv * gain[0:1, :]).astype(BF)

    @pl.when(pl.program_id(1) == 0)
    def _():
        stream[...] = value


def pick(slots, toks, gains, nch):
    _, rows, width = toks.shape
    return pl.pallas_call(
        pick_kernel,
        grid_spec=pltpu.PrefetchScalarGridSpec(
            num_scalar_prefetch=1,
            grid=(rows // HALF, nch),
            in_specs=[
                pl.BlockSpec((None, HALF, width), lambda h, k, idx: (idx[k], h, 0)),
                pl.BlockSpec((None, 8, width), lambda h, k, idx: (0, 0, 0)),
            ],
            out_specs=[
                pl.BlockSpec((None, None, HALF, width), lambda h, k, idx: (h, k, 0, 0)),
                pl.BlockSpec((None, HALF, width), lambda h, k, idx: (h, 0, 0)),
            ],
        ),
        out_shape=[struct((rows // HALF, nch, HALF, width), BF), struct((rows // HALF, HALF, width), F32)],
        name="pick",
    )(slots, toks, gains)


def hop_task(hop, arrays):
    count = lax.axis_size("rep")
    mid = count // 2
    total = len(arrays)
    inward, exchange = hop < mid - 1, hop == mid - 1
    sender = min(hop, 2 * mid - 1 - hop)
    taker = sender if exchange else sender + (1 if inward else -1)

    def copies(ins, scr):
        _, inner, outer = on_line(count)
        to = outer if hop >= mid else inner
        return [push(ins[i], scr[2 + i], scr[0], i, to) for i in range(total)]

    def start(ins, outs, scr):
        depth, _, _ = on_line(count)

        @pl.when(depth == sender)
        def _():
            for copy in copies(ins, scr):
                copy.start()

    def finish(ins, outs, scr):
        depth, _, _ = on_line(count)
        sent = copies(ins, scr)
        loads = [pltpu.make_async_copy(ins[i], scr[2 + total + i], scr[1].at[0, i]) for i in range(total)]
        stores = [pltpu.make_async_copy(scr[2 + total + i], outs[i], scr[1].at[1, i]) for i in range(total)]
        for load in loads:
            load.start()

        @pl.when(depth == sender)
        def _():
            for copy in sent:
                copy.wait_send()

        for load in loads:
            load.wait()

        @pl.when(depth == taker)
        def _():
            for i in range(total):
                sent[i].wait_recv()
                came, own = scr[2 + i], scr[2 + total + i]
                if hop >= mid:
                    own[...] = came[...]
                else:
                    own[...] = (own[...].astype(F32) + came[...].astype(F32)).astype(BF)

        for store in stores:
            store.start()
        for store in stores:
            store.wait()

    buffers = [pltpu.VMEM(array.shape, BF) for array in arrays]
    return Task(
        [(array, ANY) for array in arrays],
        [(struct(array.shape, BF), ANY) for array in arrays],
        [pltpu.SemaphoreType.DMA((2, total)), pltpu.SemaphoreType.DMA((2, total))] + buffers * 2,
        start,
        finish,
        ("inner", "outer"),
    )


def line_kernel(count, nch, items, ins, outs, scratch):
    mid = count // 2
    hops = 2 * mid - 1
    s1, r1, s2, r2, s3, r3, s4, r4, sx, core_sem, from_core = scratch[:11]
    free = list(scratch[11:])
    in1, res = [], []
    for (kind, k, done, _), mine, out in zip(items, ins, outs):
        in1.append(free.pop(0) if needs_in(kind, done, mid) else None)
        if done >= hops:
            res.append(mine)
        else:
            res.append(free.pop(0) if needs_res(kind, k) else out)
    depth, inner, outer = on_line(count)
    peers = [chip_peer(k) for k in range(nch)]
    barrier = pltpu.get_barrier_semaphore()

    def tell(device):
        pl.semaphore_signal(barrier, inc=1, device_id=device, device_id_type=pl.DeviceIdType.MESH)

    tell(inner)
    tell(core_peer())
    for k in range(1, nch):
        tell(peers[k])

    @pl.when(depth > 0)
    def _():
        tell(outer)
        pl.semaphore_wait(barrier, nch + 2)

    @pl.when(depth == 0)
    def _():
        pl.semaphore_wait(barrier, nch + 1)

    chunks = []
    for i, (kind, _, _, _) in enumerate(items):
        tall = ins[i].shape[0]
        cut = tall // 32 * 16
        chunks += [(i, 0, cut), (i, cut, tall - cut)] if kind == "block" else [(i, 0, tall)]

    def view(refs, c):
        i, lo, size = chunks[c]
        return refs[i].at[pl.ds(lo, size), :]

    def copy(src, dst, send, recv, i, device):
        return pltpu.make_async_remote_copy(
            src_ref=src,
            dst_ref=dst,
            send_sem=send.at[i],
            recv_sem=recv.at[i],
            device_id=device,
            device_id_type=pl.DeviceIdType.MESH,
        )

    def facts(c, place):
        kind, k, done, _ = items[chunks[c][0]]
        middle = place == mid - 1
        return dict(
            kind=kind,
            k=k,
            over=done >= hops,
            takes=place > 0 and place - 1 >= done,
            gives=place >= done,
            trade=middle and mid - 1 >= done,
            known=2 * mid - 2 - place < done,
            outward=place > 0 and 2 * mid - 1 - place >= done,
        )

    def sent_from(c, fact):
        return in1 if fact["takes"] or fact["kind"] == "small" else ins

    def hop1(c, fact):
        return copy(view(sent_from(c, fact), c), view(in1, c), s1, r1, c, inner)

    def hop2(c, fact):
        return copy(view(sent_from(c, fact), c), view(res, c), s2, r2, c, inner)

    def came(c, send, recv):
        return copy(view(res, c), view(res, c), send, recv, c, outer)

    def hop4(c, fact):
        i = chunks[c][0]
        if fact["kind"] == "block" and fact["k"]:
            return [copy(view(res, c), view(outs, c), s4, r4, c, peers[fact["k"]])]
        if fact["kind"] == "small":
            return [push(res[i], outs[i].at[j], sx, j, peers[j]) for j in range(1, nch)]
        return []

    small = next(i for i, item in enumerate(items) if item[0] == "small")
    to_core = push(ins[small], from_core, core_sem, 0, core_peer())
    to_core.start()

    def inward(c, fact):
        i = chunks[c][0]
        if fact["over"] or fact["known"]:
            return None
        if fact["kind"] == "small":
            to_core.wait()
            value = ins[i][...] + from_core[...]
            if fact["takes"]:
                hop1(c, fact).wait_recv()
                value = value + in1[i][...]
            in1[i][...] = value
        elif fact["takes"]:
            hop1(c, fact).wait_recv()
            value = view(ins, c)[...].astype(F32) + view(in1, c)[...].astype(F32)
            view(in1, c)[...] = value.astype(BF)
        if fact["trade"]:
            out = hop2(c, fact)
        elif fact["gives"]:
            out = hop1(c, fact)
        else:
            return None
        out.start()
        return out

    def outward(c, fact):
        i = chunks[c][0]
        if not fact["over"]:
            if fact["trade"]:
                hop2(c, fact).wait_recv()
                value = view(sent_from(c, fact), c)[...].astype(F32) + view(res, c)[...].astype(F32)
                view(res, c)[...] = value.astype(ins[i].dtype)
            elif fact["known"]:
                view(res, c)[...] = view(ins, c)[...]
            else:
                came(c, s3, r3).wait_recv()
            if fact["outward"]:
                came(c, s3, r3).start()
        if fact["kind"] == "small":
            outs[i][0] = res[i][...]
        elif fact["over"] and not hop4(c, fact):
            view(outs, c)[...] = view(ins, c)[...]
        for item in hop4(c, fact):
            item.start()

    total = len(chunks)
    for place in range(mid):

        @pl.when(depth == place)
        def _(place=place):
            lag = 2 + 3 * (mid - 1 - place)
            all_facts = [facts(c, place) for c in range(total)]
            flying = []
            for i in range(total + lag):
                if i < total:
                    if len(flying) >= 2:
                        flying.pop(0).wait_send()
                    started = inward(i, all_facts[i])
                    if started is not None:
                        flying.append(started)
                if i >= lag:
                    outward(i - lag, all_facts[i - lag])
            for item in flying:
                item.wait_send()
            for c, fact in enumerate(all_facts):
                if fact["outward"] and not fact["over"]:
                    came(c, s3, r3).wait_send()
                for item in hop4(c, fact):
                    item.wait()


def needs_in(kind, done, mid):
    return kind == "small" or done < mid - 1


def needs_res(kind, k):
    return kind == "small" or (kind == "block" and k > 0)


def line_sum(cid, nch, items):
    count = lax.axis_size("rep")
    mid = count // 2
    arrays = [item[3] for item in items]
    scratch = []
    for kind, k, done, array in items:
        if needs_in(kind, done, mid):
            scratch.append(pltpu.VMEM(array.shape, array.dtype))
        if done < 2 * mid - 1 and needs_res(kind, k):
            scratch.append(pltpu.VMEM(array.shape, array.dtype))
    total = 2 * len(items)
    small = next(array for kind, _, _, array in items if kind == "small")
    fixed = [pltpu.SemaphoreType.DMA((total,))] * 8
    fixed += [pltpu.SemaphoreType.DMA((2, nch)), pltpu.SemaphoreType.DMA((2, 1)), pltpu.VMEM(small.shape, F32)]
    vmem = pl.BlockSpec(memory_space=pltpu.VMEM)
    shapes = [
        struct(((nch,) if kind == "small" else ()) + array.shape, array.dtype) for kind, _, _, array in items
    ]

    def kernel(*refs):
        refs = list(refs)
        line_kernel(count, nch, items, refs[: len(items)], refs[len(items) : 2 * len(items)], refs[2 * len(items) :])

    return pl.pallas_call(
        kernel,
        in_specs=[vmem] * len(items),
        out_specs=[vmem] * len(items),
        out_shape=shapes,
        scratch_shapes=fixed + scratch,
        compiler_params=pltpu.CompilerParams(collective_id=cid, has_side_effects=True, vmem_limit_bytes=63 << 20),
        cost_estimate=pl.CostEstimate(flops=0, bytes_accessed=400 << 20, transcendentals=0),
        name="line_sum",
    )(*arrays)


def unpack_kernel(nch, inner, index, *refs):
    out = refs[-1]
    local = inner // nch
    step = local // HEADDIM
    for layer in range(LAYERS):

        @pl.when(pl.program_id(0) == layer)
        def _():
            blocks = refs[layer * nch : (layer + 1) * nch]
            bc = 0.0
            for k in range(nch):
                of = jnp.bitwise_xor(index[0], k)
                for j in range(2):
                    to = pl.multiple_of(of * local + j * inner, local)
                    out[0, pl.ds(to, local), :] = blocks[k][j * local : (j + 1) * local, :].astype(F32)
                bc = bc + blocks[k][2 * local : 2 * local + 2 * STATE, :].astype(F32)
                to = pl.multiple_of(of * step + 2 * inner + 2 * STATE, step)
                at = 2 * local + 2 * STATE
                out[0, pl.ds(to, step), :] = blocks[k][at : at + STEPS, :].astype(F32)[:step]
            out[0, 2 * inner : 2 * inner + 2 * STATE, :] = bc


def unpack(index, blocks, inner, columns):
    nch = len(blocks[0])
    tall, part = blocks[0][0].shape
    specs = [pl.BlockSpec((tall, part), lambda i, idx: (0, 0))] * nch
    return pl.pallas_call(
        functools.partial(unpack_kernel, nch, inner),
        grid_spec=pltpu.PrefetchScalarGridSpec(
            num_scalar_prefetch=1,
            grid=(LAYERS,),
            in_specs=specs * LAYERS,
            out_specs=pl.BlockSpec((1, columns, part), lambda i, idx: (i, 0, 0)),
        ),
        out_shape=struct((LAYERS, columns, part), F32),
        compiler_params=pltpu.CompilerParams(vmem_limit_bytes=60 << 20),
        name="unpack",
    )(index, *sum(blocks, []))


def body(
    tokens,
    lengths,
    order,
    norm_gain,
    in_proj,
    conv_weight,
    conv_bias,
    dt_bias,
    a_log,
    skip,
    gate_norm,
    out_proj,
    cotangent,
):
    n = lax.axis_size("shard")
    nch = n // 2
    me = lax.axis_index("shard")
    chip, core = me // 2, me % 2
    index = jnp.stack([chip, core]).astype(jnp.int32)
    base = lax.axis_index("rep") * n
    width = tokens.shape[2]
    inner = gate_norm.shape[1] * n
    channels = conv_bias.shape[1] * n
    local = inner // nch
    ng = local // GROUP
    rows = nch * HALF
    sizes = (norm_gain.shape[1], gate_norm.shape[1], conv_bias.shape[1], dt_bias.shape[1])
    transposed = jnp.swapaxes(in_proj, 1, 2)

    def tiled(x):
        return jnp.pad(x, ((0, 0), (0, 128 - x.shape[1])))

    def wide(x):
        return jnp.pad(x, ((0, 0),) * (x.ndim - 1) + ((0, width - x.shape[-1]),))

    top = wide(jnp.concatenate([norm_gain, gate_norm, tiled(dt_bias), tiled(a_log), tiled(skip)], 1))
    small = jnp.concatenate([top[:, None], wide(conv_weight), wide(conv_bias)[:, None]], 1)
    small = jnp.pad(small, ((0, 0), (0, 2), (0, 0))).reshape(8 * LAYERS, width)

    seqs = base + 2 * jnp.bitwise_xor(chip, jnp.arange(nch)) + core
    listing = jnp.arange(order.shape[0])
    slots = jnp.sum(jnp.where(order[None] == seqs[:, None], listing[None], 0), axis=1) - base
    slots = (jnp.bitwise_xor(core, slots % 2) * nch + jnp.bitwise_xor(chip, slots // 2)).astype(jnp.int32)
    valid = lengths[base + me]
    halves = (0, 1)
    mask = [
        jnp.broadcast_to(((jnp.arange(HALF) + h * HALF) < valid).astype(F32)[:, None], (HALF, 128)) for h in halves
    ]
    gout = [
        jnp.where(mask[h][:, 0:1] > 0, cotangent[0, h * HALF : (h + 1) * HALF], jnp.zeros((), BF)) for h in halves
    ]

    w0, toks, smalls, wo0, wo1 = start_up(transposed, tokens, small, out_proj, nch, inner, channels)
    gains, pm, pbc = make_params(index, smalls, nch, ng, sizes)
    xs, stream0 = pick(slots, toks, gains, nch)
    weights = [weight_ins(w0, wo0, pm, pbc, 0), None]

    def picked(h):
        return [(xs, pl.BlockSpec((None, None, HALF, width), lambda g, k=k: (h, k, 0, 0))) for k in range(nch)]

    def others(array, lanes=None, lane_block=0):
        return [row_of(array, k, lanes, lane_block) for k in range(nch - 1)]

    stream0 = [row_of(stream0, h) for h in halves]
    gain = [row_of(gains, layer) for layer in range(LAYERS)]
    flow1 = [(cotangent, pl.BlockSpec((None, HALF, width), lambda g, h=h: (0, h, 0))) for h in halves]

    r00, ((fetched,),) = run_fwd(
        2, picked(0), weights[0], None, [fetch_task(transposed, 1, nch, inner, channels)]
    )
    r01, ((branch00, stream10, norm10, scale00),) = run_fwd(
        3, picked(1), weights[0], r00, [owner_fwd(r00["parts"], stream0[0], mask[0], gain[1], None, inner)]
    )
    _, (near10,), (branch01, stream11, norm11, scale01), (w1,) = launch(
        "between_layers",
        4,
        1,
        None,
        [],
        [],
        [],
        [
            gather_task([norm10], nch),
            owner_fwd(r01["parts"], stream0[1], mask[1], gain[1], None, inner),
            finish_task(transposed, fetched, 1, nch, inner, channels),
        ],
    )
    weights[1] = weight_ins(w1, wo1, pm, pbc, 1)
    r10, ((near11,),) = run_fwd(5, [full(norm10)] + others(near10), weights[1], None, [gather_task([norm11], nch)])
    r11, ((branch10, out0, scal10),) = run_fwd(
        6,
        [full(norm11)] + others(near11),
        weights[1],
        r10,
        [owner_fwd(r10["parts"], full(stream10), mask[0], None, full(gout[0]), inner)],
    )
    _, (cot1, near_s0), (branch11, out1, scal11, near_s1) = launch(
        "turn",
        7,
        1,
        None,
        [],
        [],
        [],
        [
            gather_task([gout[1], scal10], nch),
            owner_fwd(r11["parts"], full(stream11), mask[1], None, full(gout[1]), inner, True),
        ],
    )
    output = jnp.concatenate([out0, out1], 0)[None]

    b11, ((cot0,),) = run_bwd(
        8,
        [full(gout[1])] + others(cot1),
        [full(scal11)] + others(near_s1),
        weights[1],
        r11,
        r10,
        None,
        [gather_task([gout[0]], nch)],
    )
    b10, ((gg11, flow11, gb01),) = run_bwd(
        9,
        [full(gout[0])] + others(cot0),
        [full(scal10)] + others(near_s0),
        weights[1],
        r10,
        None,
        b11,
        [owner_bwd(b11["parts"], full(stream11), gain[1], flow1[1], mask[1], branch01, scale01, inner)],
    )

    def flat(x):
        return x.reshape(rows, -1)

    def grads(first, second, back_a, back_b):
        pieces = [first["xall"], second["xall"]]
        for name in ("gpz", "gpx", "gpbc", "gnorm", "gall"):
            pieces += [flat(back_a[name]), flat(back_b[name])]
        return grads_task(nch, *pieces)

    _, (near_b1,), (gg10, flow10, gb00), last_grads = launch(
        "grads_last",
        10,
        1,
        None,
        [],
        [],
        [],
        [
            gather_task([gb01], nch),
            owner_bwd(b10["parts"], full(stream10), gain[1], flow1[0], mask[0], branch00, scale00, inner),
            grads(r10, r11, b10, b11),
        ],
    )
    in1, rows1 = list(last_grads[:nch]), list(last_grads[nch:])
    hops = 2 * (lax.axis_size("rep") // 2) - 1
    batches = [[in1[nch - 1 - i], rows1[i]] for i in range(3)]
    passed = [0, 0, 0]

    def hop_tasks(step):
        return [hop_task(passed[i], batches[i]) for i in range(step + 1) if passed[i] < hops]

    def hopped(step, results):
        results = list(results)
        for i in range(step + 1):
            if passed[i] < hops:
                batches[i] = list(results.pop(0))
                passed[i] += 1

    def payload(own, near):
        tile = width // 128
        gs = [(own, pl.BlockSpec((HALF, width), lambda g: (0, 0)))] + others(near, width)
        ts = [(own, pl.BlockSpec((HALF, 128), lambda g: (0, tile)))] + others(near, 128, tile)
        return gs, ts

    b01, ((near_b0,), *more) = run_bwd(
        11, *payload(gb01, near_b1), weights[0], r01, r00, None, [gather_task([gb00], nch)] + hop_tasks(0)
    )
    hopped(0, more)
    b00, ((gg01, gtok1), *more) = run_bwd(
        12,
        *payload(gb00, near_b0),
        weights[0],
        r00,
        None,
        b01,
        [owner_bwd(b01["parts"], stream0[1], gain[0], full(flow11), None, None, None, inner)] + hop_tasks(1),
    )
    hopped(1, more)
    _, (gg00, gtok0), first_grads, *more = launch(
        "grads_first",
        13,
        1,
        None,
        [],
        [],
        [],
        [
            owner_bwd(b00["parts"], stream0[0], gain[0], full(flow10), None, None, None, inner),
            grads(r00, r01, b00, b01),
        ]
        + hop_tasks(2),
    )
    hopped(2, more)
    in0, rows0 = list(first_grads[:nch]), list(first_grads[nch:])
    grad_tokens = jnp.concatenate([gtok0, gtok1], 0)[None]

    def packed(a, b, ga, gb):
        bc = a["sgbc"] + b["sgbc"]
        tail = jnp.pad(bc[:, 2 * STATE :], ((0, 0), (0, GROUP - STATE)))
        return [(a["sgm"] + b["sgm"]).reshape(8 * ng, GROUP), bc[:, : 2 * STATE], tail, (ga + gb)[0].reshape(-1, GROUP)]

    vectors = jnp.concatenate(packed(b00, b01, gg00, gg01) + packed(b10, b11, gg10, gg11), 0)
    for i in range(3):
        in1[nch - 1 - i], rows1[i] = batches[i]
    items = []
    for i in range(3):
        items += [("block", nch - 1 - i, passed[i], in1[nch - 1 - i]), ("rows", 0, passed[i], rows1[i])]
    items += [("block", k, 0, in1[k]) for k in range(nch - 4, -1, -1)] + [("rows", 0, 0, rows1[3])]
    items += [("block", k, 0, in0[k]) for k in range(nch - 1, 0, -1)] + [("small", 0, 0, vectors)]
    items += [("block", 0, 0, in0[0])] + [("rows", 0, 0, item) for item in rows0]
    summed = line_sum(14, nch, items)
    sums = summed[items.index(next(item for item in items if item[0] == "small"))]

    def result(array):
        return next(out for item, out in zip(items, summed) if item[3] is array)

    in0, in1 = [result(item) for item in in0], [result(item) for item in in1]
    rows0 = jnp.concatenate([result(item) for item in rows0], 0)
    rows1 = jnp.concatenate([result(item) for item in rows1], 0)
    grads_in = jnp.swapaxes(unpack(index, [in0, in1], inner, in_proj.shape[2]), 1, 2)
    grads_out = jnp.stack([rows0, rows1]).astype(F32)

    sums = jnp.stack([lax.dynamic_index_in_dim(sums, jnp.bitwise_xor(chip, q), 0, keepdims=False) for q in range(nch)])
    sums = sums.reshape(nch, LAYERS, -1, GROUP)
    main = sums[:, :, : 8 * ng].reshape(nch, LAYERS, ng, 8, GROUP).transpose(1, 3, 0, 2, 4)
    main = main.reshape(LAYERS, 8, inner)
    bc = sums[:, :, 8 * ng : 8 * ng + 8].sum(0)
    steps = sums[:, :, 8 * ng + 8 : 8 * ng + 16, : local // HEADDIM].transpose(1, 2, 0, 3).reshape(LAYERS, 8, -1)
    grad_gain = sums[:, :, 8 * ng + 16 :].sum(0).reshape(LAYERS, width)
    conv = jnp.concatenate([main[:, :5], bc[:, :5]], 2)
    skips = main[:, 5].reshape(LAYERS, -1, HEADDIM).sum(-1)

    def own(x):
        part = x.shape[-1] // n
        return lax.dynamic_slice_in_dim(x, me * part, part, x.ndim - 1)

    conv = own(conv)
    return (
        output,
        grad_tokens,
        own(grad_gain),
        grads_in,
        conv[:, :4],
        conv[:, 4],
        own(steps[:, 4]),
        own(steps[:, 5]),
        own(skips),
        own(main[:, 6]),
        grads_out,
    )


def solution(mesh):
    in_specs = (
        P(("rep", "shard"), None, None),
        P(),
        P(),
        P(None, "shard"),
        P(None, "shard", None),
        P(None, None, "shard"),
        P(None, "shard"),
        P(None, "shard"),
        P(None, "shard"),
        P(None, "shard"),
        P(None, "shard"),
        P(None, "shard", None),
        P(("rep", "shard"), None, None),
    )
    out_specs = (
        P(("rep", "shard"), None, None),
        P(("rep", "shard"), None, None),
        P(None, "shard"),
        P(None, "shard", None),
        P(None, None, "shard"),
        P(None, "shard"),
        P(None, "shard"),
        P(None, "shard"),
        P(None, "shard"),
        P(None, "shard"),
        P(None, "shard", None),
    )
    return jax.shard_map(body, mesh=mesh, in_specs=in_specs, out_specs=out_specs, check_vma=False)
```

time: 2250 us -> 989 us (0.44)
  waiting for transfers between devices: 1130 us -> 0 us
  Pallas kernels: 0 us -> 944 us
  matrix products: 451 us -> 0 us
  local copies, waits for them, and re-layouts: 298 us -> 20.4 us
  other arithmetic: 189 us -> 14.5 us
  blocking collectives: 145 us -> 0 us
    pallas_call x0 -> x17, Pallas kernels: none -> 944 us  [the longest x12 562 us: launch(): pl.pallas_call(kernel, grid=(steps,), in_specs=[spec for _, spec in all_i...]
    all_gather x15 -> x0, waiting for transfers between devices: 656 us -> none  [the longest x2 342 us: reduce_grads(): proj_piece = lax.all_gather(grad_proj, 'shard', axis=0, tiled=True)]
    dot_general x38 -> x0, matrix products: 451 us -> none  [the longest x8 181 us: block_step(): intra = jnp.einsum('tsh,shp->thp', weights, inputs_b, precision=HIGH)]
    psum x1 -> x0, waiting for transfers between devices: 440 us -> none  [reduce_grads(): lax.psum(parted[1].astype(jnp.bfloat16), 'rep').astype(jnp.float32)]
    slice x16 -> x7, local copies, waits for them, and re-layouts: 220 us -> 0.04 us  [the longest x2 0.02 us: body(): conv = jnp.concatenate([main[:, :5], bc[:, :5]], 2)]
    all_gather x6 -> x0, blocking collectives: 75.4 us -> none  [the longest x2 41.9 us: fetch_forward(): lax.all_gather(pieces[2], 'shard', axis=1, tiled=True)]
    reduce_sum x16 -> x3, other arithmetic: 68.5 us -> 0.29 us  [the longest x1 0.18 us: body(): jnp.sum(jnp.where(order[None] == seqs[:, None], listing[None], 0), axis=1)]
    unnamed x2 -> x0, blocking collectives: 50.8 us -> none
  transfers between devices with their start and end apart: 18 -> 0, of which waited for: 10 -> 0; matrix products, arithmetic and copies ran while one was open for 32% -> 0% of each run, Pallas kernels for 0% -> 0%
where the time goes in v1:
time: 989 us; the launch traced here: 981 us
  Pallas kernels  944 us (95%)
  local copies, waits for them, and re-layouts  20.4 us (2%)
  other arithmetic  14.5 us (1%)
    pallas_call x12, Pallas kernels, launch(): pl.pallas_call(kernel, grid=(steps,), in_specs=[spec for _, spec in all_i...  562 us
    pallas_call x1, Pallas kernels, line_sum(): pl.pallas_call(kernel, in_specs=[vmem] * len(items), out_specs=[vmem] * l...  277 us
    pallas_call x1, Pallas kernels, start_up(): pl.pallas_call(functools.partial(start_kernel, nch, inner, channels), in_...  83.3 us

profile of v1, /device:TPU:0, one launch (start us, length us, event | category | flops | bytes accessed | tf_op | source)
XLA Modules:
  0.0 980.9 jit_solution(7141455671776695268)
XLA Ops:
  6.2 2.2 copy-done.2
  8.3 1.2 copy-done.3
  9.6 83.3 %start_up.1 = (bf16[2,8,1168,256]{3,2,1,0:T(8,128)(2,1)}, bf16[8,256,2048]{2,1,0:T(8,128)(2,1)}, bf16[8,16,2048]{2,1,0:T(8,128)(2,1)S(1)}, bf16[1024,2048]{1,0:T(8,128)(2,1)S(1)}, bf16[1024,2048]{1,0:T(8,128)(2,1)S(1)}) custom-call(bf16[2,8512,256]{2,1,0:T(8,128)(2,1)} %bitcast.68, bf16[1,256,2048]{2,1,0:T(8,128)(2,1)S(1)} %copy-done.3, ...), custom_call_target="tpu_custom_call" | custom-call | tf_op jit(solution)/shard_map/start_up/pallas_call | solution.py:1071
  92.9 2.0 copy-done
  94.9 2.0 copy-done.1
  97.7 2.6 params.1
  101.0 8.7 pick.1
  109.7 35.9 %fwd_first.2 = (bf16[4,128,2176]{2,1,0:T(8,128)(2,1)}, bf16[512,2048]{1,0:T(8,128)(2,1)}, f32[4,128,1024]{2,1,0:T(8,128)}, f32[4,128,1024]{2,1,0:T(8,128)}, f32[...) custom-call(bf16[2,4,128,2048]{3,2,1,0:T(8,128)(2,1)} %get-tuple-element., ...), custom_call_target="tpu_custom_call" | custom-call | flops 14495514624 | bytes 41943040 | tf_op jit(solution)/shard_map/fwd_first/pallas_call | solution.py:584
  147.5 36.7 %fwd_second.2 = (bf16[4,128,2176]{2,1,0:T(8,128)(2,1)}, bf16[512,2048]{1,0:T(8,128)(2,1)}, f32[4,128,1024]{2,1,0:T(8,128)}, f32[4,128,1024]{2,1,0:T(8,128)}, f32...) custom-call(bf16[2,4,128,2048]{3,2,1,0:T(8,128)(2,1)} %get-tuple-ele, ...), custom_call_target="tpu_custom_call" | custom-call | flops 14495514624 | bytes 41943040 | tf_op jit(solution)/shard_map/fwd_second/pallas_call | solution.py:584
  185.0 55.2 %between_layers.1 = (bf16[3,128,2048]{2,1,0:T(8,128)(2,1)}, f32[128,2048]{1,0:T(8,128)}, f32[128,2048]{1,0:T(8,128)}, bf16[128,2048]{1,0:T(8,128)(2,1)}, f32[128...) custom-call(bf16[128,2048]{1,0:T(8,128)(2,1)} %get-tuple-element.175.refs_0_, ...), custom_call_target="tpu_custom_call" | custom-call | bytes 41943040 | tf_op jit(solution)/shard_map/between_layers/pallas_call | solution.py:584
  240.2 30.8 %fwd_first.3 = (bf16[4,128,2176]{2,1,0:T(8,128)(2,1)}, bf16[512,2048]{1,0:T(8,128)(2,1)}, f32[4,128,1024]{2,1,0:T(8,128)}, f32[4,128,1024]{2,1,0:T(8,128)}, f32[...) custom-call(bf16[128,2048]{1,0:T(8,128)(2,1)} %get-tuple-element.175.refs, ...), custom_call_target="tpu_custom_call" | custom-call | flops 14495514624 | bytes 41943040 | tf_op jit(solution)/shard_map/fwd_first/pallas_call | solution.py:584
  271.6 1.1 bitcast_select_fusion.1
  272.7 34.9 %fwd_second.3 = (bf16[4,128,2176]{2,1,0:T(8,128)(2,1)}, bf16[512,2048]{1,0:T(8,128)(2,1)}, f32[4,128,1024]{2,1,0:T(8,128)}, f32[4,128,1024]{2,1,0:T(8,128)}, f32...) custom-call(bf16[128,2048]{1,0:T(8,128)(2,1)} %get-tuple-element.178, ...), custom_call_target="tpu_custom_call" | custom-call | flops 14495514624 | bytes 41943040 | tf_op jit(solution)/shard_map/fwd_second/pallas_call | solution.py:584
  307.6 58.5 %turn.1 = (bf16[3,128,2048]{2,1,0:T(8,128)(2,1)}, bf16[3,128,128]{2,1,0:T(8,128)(2,1)}, f32[128,2048]{1,0:T(8,128)}, bf16[128,2048]{1,0:T(8,128)(2,1)}, bf16[128...) custom-call(bf16[128,2048]{1,0:T(8,128)(2,1)} %get-tuple-element.349.refs_0_.refs_6_, ...), custom_call_target="tpu_custom_call" | custom-call | bytes 41943040 | tf_op jit(solution)/shard_map/turn/pallas_call | solution.py:584
  366.1 32.9 %bwd_second.2 = (bf16[4,128,2048]{2,1,0:T(8,128)(2,1)}, bf16[512,2048]{1,0:T(8,128)(2,1)}, bf16[4,128,1024]{2,1,0:T(8,128)(2,1)}, bf16[4,128,1024]{2,1,0:T(8,128...) custom-call(bf16[128,2048]{1,0:T(8,128)(2,1)} %get-tuple-element.349, ...), custom_call_target="tpu_custom_call" | custom-call | flops 28991029248 | bytes 41943040 | tf_op jit(solution)/shard_map/bwd_second/pallas_call | solution.py:584
  399.0 40.6 %bwd_first.2 = (bf16[4,128,2048]{2,1,0:T(8,128)(2,1)}, bf16[512,2048]{1,0:T(8,128)(2,1)}, bf16[4,128,1024]{2,1,0:T(8,128)(2,1)}, bf16[4,128,1024]{2,1,0:T(8,128)...) custom-call(bf16[128,2048]{1,0:T(8,128)(2,1)} %get-tuple-element.348, ...), custom_call_target="tpu_custom_call" | custom-call | flops 28991029248 | bytes 41943040 | tf_op jit(solution)/shard_map/bwd_first/pallas_call | solution.py:584
  439.6 61.3 %grads_last.1 = (bf16[3,128,2176]{2,1,0:T(8,128)(2,1)}, f32[8,2048]{1,0:T(8,128)}, f32[128,2048]{1,0:T(8,128)}, bf16[128,2176]{1,0:T(8,128)(2,1)}, bf16[2320,256...) custom-call(bf16[128,2176]{1,0:T(8,128)(2,1)} %get-tuple-element.210, ...), custom_call_target="tpu_custom_call" | custom-call | bytes 41943040 | tf_op jit(solution)/shard_map/grads_last/pallas_call | solution.py:584
  501.9 49.9 %bwd_second.3 = (bf16[4,128,2048]{2,1,0:T(8,128)(2,1)}, bf16[512,2048]{1,0:T(8,128)(2,1)}, bf16[4,128,1024]{2,1,0:T(8,128)(2,1)}, bf16[4,128,1024]{2,1,0:T(8,128...) custom-call(bf16[128,2176]{1,0:T(8,128)(2,1)} %get-tuple-element.210, ...), custom_call_target="tpu_custom_call" | custom-call | flops 28991029248 | bytes 41943040 | tf_op jit(solution)/shard_map/bwd_second/pallas_call | solution.py:584
  551.9 51.3 %bwd_first.3 = (bf16[4,128,2048]{2,1,0:T(8,128)(2,1)}, bf16[512,2048]{1,0:T(8,128)(2,1)}, bf16[4,128,1024]{2,1,0:T(8,128)(2,1)}, bf16[4,128,1024]{2,1,0:T(8,128)...) custom-call(bf16[128,2176]{1,0:T(8,128)(2,1)} %get-tuple-element.226, ...), custom_call_target="tpu_custom_call" | custom-call | flops 28991029248 | bytes 41943040 | tf_op jit(solution)/shard_map/bwd_first/pallas_call | solution.py:584
  603.3 73.7 %grads_first.1 = (f32[8,2048]{1,0:T(8,128)}, bf16[128,2048]{1,0:T(8,128)(2,1)}, bf16[2320,256]{1,0:T(8,128)(2,1)}, bf16[2320,256]{1,0:T(8,128)(2,1)}, bf16[2320,...) custom-call(bf16[4,128,2048]{2,1,0:T(8,128)(2,1)} %get-tuple-element, ...), custom_call_target="tpu_custom_call" | custom-call | bytes 41943040 | tf_op jit(solution)/shard_map/grads_first/pallas_call | solution.py:584
  678.7 276.6 %line_sum.1 = (bf16[2320,256]{1,0:T(8,128)(2,1)}, bf16[128,2048]{1,0:T(8,128)(2,1)}, bf16[2320,256]{1,0:T(8,128)(2,1)}, bf16[128,2048]{1,0:T(8,128)(2,1)}, bf16[...) custom-call(bf16[2320,256]{1,0:T(8,128)(2,1)} %get-tuple-element.268, ...), custom_call_target="tpu_custom_call" | custom-call | bytes 419430400 | tf_op jit(solution)/shard_map/line_sum/pallas_call | solution.py:1534
  955.3 1.8 maximum_bitcast_fusion
  957.6 3.9 maximum_convert_fusion
  963.4 11.5 %unpack.1 = f32[2,8512,256]{2,1,0:T(8,128)} custom-call(s32[2]{0:T(128)} %pad_add_fusion.index, bf16[2320,256]{1,0:T(8,128)(2,1)} %get-tuple-element.297.refs_0_, bf16[2320,256]{1,0:T(8,128)(2,1)} %get-tuple-element.298.refs_1_, bf16[2320,256]{1,0:T(8,128)(2,1)} %get-tuple-element.299.refs_2_, bf16[2320,256]{1,0:T(8,128)(2,1)} %get-tuple-element.300.refs_3_, ...), custom_call_target="tpu_custom_call" | custom-call | tf_op jit(solution)/shard_map/unpack/pallas_call | solution.py:1572
  (112 shorter events, 20.6 us)
Async XLA Ops:
  6.1 2.2 copy-start.2
  8.3 1.2 copy-start.3
  9.6 90.7 %copy-start.24 = (s32[32]{0:T(128)S(1)}, s32[32]{0:T(128)}, u32[]{:S(2)}) copy-start(s32[32]{0:T(128)} %param.15) | copy-start | bytes 388
  92.8 2.0 copy-start
  94.9 2.0 copy-start.1
  109.7 35.9 %copy-start.25 = (s32[32]{0:T(128)S(1)}, s32[32]{0:T(128)}, u32[]{:S(2)}) copy-start(s32[32]{0:T(128)} %param.14) | copy-start | bytes 388
  240.2 31.5 %copy-start.5 = (bf16[1,256,2048]{2,1,0:T(8,128)(2,1)S(1)}, bf16[1,256,2048]{2,1,0:T(8,128)(2,1)}, u32[]{:S(2)}) copy-start(bf16[1,256,2048]{2,1,0:T(8,128)(2,1)} %refs_5_.1) | copy-start | bytes 3145732
  439.6 62.3 %copy-start.21 = (f32[8,384]{1,0:T(8,128)S(1)}, f32[8,384]{1,0:T(8,128)}, u32[]{:S(2)}) copy-start(f32[8,384]{1,0:T(8,128)} %get-tuple-element.288) | copy-start | bytes 36868
  439.6 62.3 %copy-start.23 = (f32[8,384]{1,0:T(8,128)S(1)}, f32[8,384]{1,0:T(8,128)}, u32[]{:S(2)}) copy-start(f32[8,384]{1,0:T(8,128)} %get-tuple-element.287) | copy-start | bytes 36868
  603.2 74.7 %copy-start.20 = (f32[8,384]{1,0:T(8,128)S(1)}, f32[8,384]{1,0:T(8,128)}, u32[]{:S(2)}) copy-start(f32[8,384]{1,0:T(8,128)} %get-tuple-element.282) | copy-start | bytes 36868
  603.2 74.7 %copy-start.22 = (f32[8,384]{1,0:T(8,128)S(1)}, f32[8,384]{1,0:T(8,128)}, u32[]{:S(2)}) copy-start(f32[8,384]{1,0:T(8,128)} %get-tuple-element.281) | copy-start | bytes 36868
  603.2 74.7 %copy-start.18 = (f32[4,8,256]{2,1,0:T(8,128)S(1)}, f32[4,8,256]{2,1,0:T(8,128)}, u32[]{:S(2)}) copy-start(f32[4,8,256]{2,1,0:T(8,128)} %get-tuple-element.280) | copy-start | bytes 98308
  603.2 74.7 %copy-start.19 = (f32[4,8,256]{2,1,0:T(8,128)S(1)}, f32[4,8,256]{2,1,0:T(8,128)}, u32[]{:S(2)}) copy-start(f32[4,8,256]{2,1,0:T(8,128)} %get-tuple-element.279) | copy-start | bytes 98308
  603.3 74.7 %copy-start.16 = (f32[4,8,256]{2,1,0:T(8,128)S(1)}, f32[4,8,256]{2,1,0:T(8,128)}, u32[]{:S(2)}) copy-start(f32[4,8,256]{2,1,0:T(8,128)} %get-tuple-element.286) | copy-start | bytes 98308
  603.3 74.7 %copy-start.17 = (f32[4,8,256]{2,1,0:T(8,128)S(1)}, f32[4,8,256]{2,1,0:T(8,128)}, u32[]{:S(2)}) copy-start(f32[4,8,256]{2,1,0:T(8,128)} %get-tuple-element.285) | copy-start | bytes 98308
  955.3 1.8 copy-start.10
  955.3 1.8 copy-start.11
  955.3 2.0 copy-start.12
  955.3 2.1 copy-start.13
  957.6 4.0 copy-start.14
  963.4 15.0 %copy-start.8 = (bf16[128,2048]{1,0:T(8,128)(2,1)S(1)}, bf16[128,2048]{1,0:T(8,128)(2,1)}, u32[]{:S(2)}) copy-start(bf16[128,2048]{1,0:T(8,128)(2,1)} %get-tuple-element.267) | copy-start | bytes 1572868
  963.4 15.0 %copy-start.9 = (bf16[128,2048]{1,0:T(8,128)(2,1)S(1)}, bf16[128,2048]{1,0:T(8,128)(2,1)}, u32[]{:S(2)}) copy-start(bf16[128,2048]{1,0:T(8,128)(2,1)} %get-tuple-element.266) | copy-start | bytes 1572868
  974.9 4.5 copy-start.6
  974.9 4.5 copy-start.7
  (2 other events, 1.4 us)
